TPU v7x, 512 devices: a whole 4x8x8 slice. The times are simulated.
512 devices in a mesh: dp: 32 (over x, y), passage: 16 (over z, core).
Axes of the slice: x: 4, y: 8, z: 8, core: 2. Of those that a mesh axis runs over, the one named last changes fastest.
Arguments:
- hidden: bfloat16 [2048, 32, 768], P(('dp', 'passage')), may hold values from -6 to 6
- weight: bfloat16 [768, 128], P('passage'), may hold values from -0.21875 to 0.21875
- cache: bfloat16 [256, 180, 128], P('passage'), may hold values from -20 to 20
- lengths: int32 [256], P('passage'), may hold values from 8 to 180, as said below
- passage_ids: int32 [2048, 16], P(('dp', 'passage')), may hold values from 0 to 255, as said below
- owner_map: int32 [256], replicated, may hold values from 0 to 255, as said below
Outputs:
- hidden_grad: bfloat16 [2048, 32, 768], P(('dp', 'passage'))
- weight_grad: float32 [768, 128], P('passage')
- cache_grad: bfloat16 [256, 180, 128], P('passage')
Inputs may be any that keep to these rules, and one draw needn't show every extreme that they name: `owner_map`: A permutation: each cache row belongs to exactly one passage id. Cache row r lies on index r // 16 of passage. `passage_ids`: among the 64 candidates of the queries of one device (aligned blocks of 4 queries), at most 12 have their cache row on any one index of passage; in every draw some index receives exactly 12 from each device of a group along passage. Ids may repeat within a query. `lengths`: cache row 0 has all 180 tokens live.
All inputs are finite; a program needn't handle non-finite values.
Results may differ from a plain program's by a relative error of at most 0.015.
The roundings to bfloat16 on the way count: a program that leaves them out, or rounds other values in their place, can miss the bound.
Values may be sent and summed in bfloat16 or wider, within the bound.
A program may use at most 64 MiB of HBM per device.

v0:
```python
import math

import jax
import jax.numpy as jnp
from jax import lax
from jax.sharding import PartitionSpec as P

TAU = 0.1
EPS = 1e-06


def tile_scores(cache, lengths, query_block, slot_block, similarity_scale):
    safe_slot = jnp.maximum(slot_block, 0)
    passage_tiles = cache[safe_slot]
    positions = jnp.arange(cache.shape[1], dtype=jnp.int32)
    valid = positions[None, :] < lengths[safe_slot][:, None]
    similarity_values = (
        jnp.einsum("cqd,cpd->cqp", query_block, passage_tiles, preferred_element_type=jnp.float32)
        * similarity_scale
    )
    masked = jnp.where(valid[:, None, :], similarity_values, -jnp.inf)
    return (passage_tiles, safe_slot, masked)


def owner_forward(cache, lengths, slot_queries, slot_ids, similarity_scale):

    def one_source(item):
        query_block, slot_block = item
        passage_tiles, safe_slot, masked = tile_scores(
            cache, lengths, query_block, slot_block, similarity_scale
        )
        row_top = jnp.max(masked, axis=-1, keepdims=True)
        log_total = row_top[..., 0] + jnp.log(jnp.sum(jnp.exp(masked - row_top), axis=-1))
        return (log_total, TAU * jnp.sum(log_total, axis=-1))

    return lax.map(one_source, (slot_queries, slot_ids))


def owner_backward(
    cache, lengths, slot_queries, slot_ids, log_totals, slot_grads, similarity_scale, root_scale
):

    def one_source(accum, item):
        query_block, slot_block, total_block, grad_block = item
        passage_tiles, safe_slot, masked = tile_scores(
            cache, lengths, query_block, slot_block, similarity_scale
        )
        probs = jnp.exp(masked - total_block[..., None])
        weight_halfwidth = (grad_block[:, None, None] * probs * root_scale).astype(jnp.bfloat16)
        query_gradient = jnp.einsum(
            "cqp,cpd->cqd", weight_halfwidth, passage_tiles, preferred_element_type=jnp.float32
        )
        passage_tile_gradient = jnp.einsum(
            "cqp,cqd->cpd", weight_halfwidth, query_block, preferred_element_type=jnp.float32
        )
        return (accum.at[safe_slot].add(passage_tile_gradient), query_gradient)

    start = jnp.zeros(cache.shape, jnp.float32)
    return lax.scan(one_source, start, (slot_queries, slot_ids, log_totals, slot_grads))


def shards(hidden, weight, cache, lengths, passage_ids, owner_map):
    owners = lax.axis_size("passage")
    query_count, query_len, model_width = hidden.shape
    pass_count, tile_len, feat_width = cache.shape
    cand_count = passage_ids.shape[1]
    capacity = 3 * query_count * cand_count // owners
    similarity_scale = 1.0 / (TAU * math.sqrt(feat_width))
    root_scale = 1.0 / math.sqrt(feat_width)
    first_one = (jnp.arange(cand_count) == 0).astype(jnp.float32)
    full_weight = lax.all_gather(weight, "passage", axis=0, tiled=True)
    query_raw = jnp.dot(
        hidden.reshape(query_count * query_len, model_width),
        full_weight,
        preferred_element_type=jnp.float32,
    ).reshape(query_count, query_len, feat_width)
    inverse_rms = lax.rsqrt(jnp.mean(query_raw * query_raw, axis=-1, keepdims=True) + EPS)
    query_vectors = (query_raw * inverse_rms).astype(jnp.bfloat16)
    cache_rows = owner_map[passage_ids]
    flat_owner = (cache_rows // pass_count).reshape(-1)
    flat_slot = (cache_rows % pass_count).reshape(-1)
    owner_hits = (flat_owner[:, None] == jnp.arange(owners)[None, :]).astype(jnp.int32)
    owner_rank = jnp.sum((jnp.cumsum(owner_hits, axis=0) - 1) * owner_hits, axis=1)
    position = flat_owner * capacity + owner_rank
    pair_queries = jnp.repeat(query_vectors, cand_count, axis=0)
    send_queries = (
        jnp.zeros((owners * capacity, query_len, feat_width), jnp.bfloat16)
        .at[position]
        .set(pair_queries)
    )
    send_slots = jnp.full((owners * capacity,), -1, jnp.int32).at[position].set(flat_slot)
    slot_queries, slot_ids = (
        lax.all_to_all(
            send_queries.reshape(owners, capacity, query_len, feat_width),
            "passage",
            split_axis=0,
            concat_axis=0,
            tiled=True,
        ),
        lax.all_to_all(
            send_slots.reshape(owners, capacity), "passage", split_axis=0, concat_axis=0, tiled=True
        ),
    )
    log_totals, slot_scores = owner_forward(
        cache, lengths, slot_queries, slot_ids, similarity_scale
    )
    back_scores = lax.all_to_all(slot_scores, "passage", split_axis=0, concat_axis=0, tiled=True)
    pair_scores = back_scores.reshape(-1)[position].reshape(query_count, cand_count)
    score_grad = jax.nn.softmax(pair_scores, axis=-1) - first_one
    send_grads = (
        jnp.zeros((owners * capacity,), jnp.float32).at[position].set(score_grad.reshape(-1))
    )
    slot_grads = lax.all_to_all(
        send_grads.reshape(owners, capacity), "passage", split_axis=0, concat_axis=0, tiled=True
    )
    cache_accum, slot_query_grads = owner_backward(
        cache, lengths, slot_queries, slot_ids, log_totals, slot_grads, similarity_scale, root_scale
    )
    back_grads = lax.all_to_all(
        slot_query_grads, "passage", split_axis=0, concat_axis=0, tiled=True
    )
    gathered_grads = back_grads.reshape(owners * capacity, query_len, feat_width)[position]
    query_gradient = jnp.sum(
        gathered_grads.reshape(query_count, cand_count, query_len, feat_width), axis=1
    )
    cache_total = lax.psum(cache_accum, "dp")
    mean_term = jnp.mean(query_gradient * query_raw, axis=-1, keepdims=True)
    cube_rms = inverse_rms * inverse_rms * inverse_rms
    raw_grad = (inverse_rms * query_gradient - query_raw * cube_rms * mean_term).astype(
        jnp.bfloat16
    )
    flat_raw = raw_grad.reshape(query_count * query_len, feat_width)
    hidden_grad = jnp.dot(flat_raw, full_weight.T, preferred_element_type=jnp.float32).astype(
        jnp.bfloat16
    )
    weight_term = jnp.einsum(
        "nd,ne->de",
        hidden.reshape(query_count * query_len, model_width),
        flat_raw,
        preferred_element_type=jnp.float32,
    )
    weight_total = lax.psum(weight_term, ("dp", "passage"))
    row_share = model_width // owners
    weight_grad = lax.dynamic_slice_in_dim(
        weight_total, lax.axis_index("passage") * row_share, row_share, 0
    )
    return (
        hidden_grad.reshape(query_count, query_len, model_width),
        weight_grad,
        cache_total.astype(jnp.bfloat16),
    )


def solution(mesh):
    in_specs = (
        P(("dp", "passage"), None, None),
        P("passage", None),
        P("passage", None, None),
        P("passage"),
        P(("dp", "passage"), None),
        P(),
    )
    out_specs = (P(("dp", "passage"), None, None), P("passage", None), P("passage", None, None))
    return jax.shard_map(shards, mesh=mesh, in_specs=in_specs, out_specs=out_specs, check_vma=False)
```

profile of v0, /device:TPU:1, one launch (start us, length us, event | category | flops | bytes accessed | tf_op | source)
XLA Modules:
  0.0 776.5 jit_solution(4750258327852608311)
XLA Ops:
  8.0 1.5 gather_fusion.4
  11.3 11.8 %all-to-all-start = ((s32[16,1,12]{2,1,0:T(1,128)}), s32[16,1,12]{2,1,0:T(1,128)S(1)}, u32[]{:S(2)}, u32[]{:S(2)}) async-start(s32[16,1,12]{2,1,0:T(1,128)} %bitcast.13), calls=%async_computation | async-start | bytes 16384 | tf_op jit(solution)/shard_map/all_to_all | solution.py:100
  23.2 17.7 %all_gather.3 = bf16[768,128]{1,0:T(8,128)(2,1)S(1)} all-gather(bf16[48,128]{1,0:T(8,128)(2,1)S(1)} %copy-done.4), channel_id=1, replica_groups=mesh['dp'=32,'passage'=16] {'passage'}, dimensions={0}, use_global_device_ids=true | all-gather | bytes 208896 | tf_op jit(solution)/shard_map/all_gather | solution.py:71
  42.7 7.1 scatter_fusion.1
  49.9 4.9 all-to-all-start.1
  55.0 38.3 %all-to-all-done.1 = bf16[16,12,32,128]{3,2,1,0:T(8,128)(2,1)} async-done(((bf16[16,12,32,128]{3,2,1,0:T(8,128)(2,1)}), bf16[16,12,32,128]{3,2,1,0:T(8,128)(2,1)}, u32[]{:S(2)}, u32[]{:S(2)}) %all-to-all-start.1) | async-done | bytes 1572896 | tf_op jit(solution)/shard_map/all_to_all | solution.py:93
  93.3 72.8 %while.24 = (s32[]{:T(128)}, f32[16,12,32]{2,1,0:T(8,128)S(1)}, f32[16,12]{1,0:T(8,128)}, s32[16,12]{1,0:T(8,128)S(1)}, s32[16]{0:T(128)S(1)}, /*index=5*/bf16[1...) while((s32[]{:T(128)}, f32[16,12,32]{2,1,0:T(8,128)S(1)}, ...), condition=%wide.region_9.10_spmd, body=%wide.region_5.9_spmd.sunk | while | flops 18043900 | bytes 2352057 | solution.py:36
  94.7 1.4 fusion.60
  99.2 1.4 fusion.60
  103.8 1.4 fusion.60
  108.3 1.4 fusion.60
  112.9 1.4 fusion.60
  117.4 1.4 fusion.60
  122.0 1.4 fusion.60
  126.6 1.4 fusion.60
  131.1 1.4 fusion.60
  135.7 1.4 fusion.60
  140.2 1.4 fusion.60
  144.7 1.4 fusion.60
  149.3 1.4 fusion.60
  153.9 1.4 fusion.60
  158.4 1.4 fusion.60
  163.0 1.4 fusion.60
  166.1 4.3 all-to-all-start.2
  170.4 6.8 all-to-all-done.2
  181.6 3.9 all-to-all-start.3
  185.5 7.0 all-to-all-done.3
  193.7 141.9 %while.25 = (s32[]{:T(128)}, f32[16,180,128]{2,1,0:T(8,128)}, f32[16,12,32,128]{3,2,1,0:T(8,128)}, s32[16,12]{1,0:T(8,128)S(1)}, f32[16,12]{1,0:T(8,128)S(1)}, /...) while((s32[]{:T(128)}, f32[16,180,128]{2,1,0:T(8,128)}, ...), condition=%wide.region_15.16_spmd, body=%wide.region_13.15_spmd.sunk | while | flops 53778556 | bytes 7458705 | solution.py:59
  197.5 1.4 fusion.71
  198.9 3.7 scatter_fusion
  206.4 1.4 fusion.71
  207.8 3.6 scatter_fusion
  215.3 1.4 fusion.71
  216.7 3.6 scatter_fusion
  224.1 1.4 fusion.71
  225.5 3.7 scatter_fusion
  233.0 1.4 fusion.71
  234.4 3.7 scatter_fusion
  241.9 1.4 fusion.71
  243.3 3.7 scatter_fusion
  250.8 1.4 fusion.71
  252.2 3.6 scatter_fusion
  259.6 1.4 fusion.71
  261.0 3.6 scatter_fusion
  268.4 1.4 fusion.71
  269.8 3.6 scatter_fusion
  277.3 1.4 fusion.71
  278.7 3.6 scatter_fusion
  286.1 1.4 fusion.71
  287.5 3.7 scatter_fusion
  295.0 1.4 fusion.71
  296.4 3.6 scatter_fusion
  303.9 1.4 fusion.71
  305.3 3.7 scatter_fusion
  312.9 1.4 fusion.71
  314.3 3.5 scatter_fusion
  321.6 1.4 fusion.71
  323.0 3.7 scatter_fusion
  330.5 1.4 fusion.71
  331.9 3.7 scatter_fusion
  335.6 4.5 all-to-all-start.4
  341.6 136.4 %all-reduce.4 = bf16[16,180,128]{2,0,1:T(8,128)(2,1)} all-reduce(f32[16,180,128]{2,0,1:T(8,128)} %copy.22), channel_id=1, replica_groups=mesh['dp'=32,'passage'=16] {'dp'}, use_global_device_ids=true, to_apply=%region_19.20 | all-reduce | flops 368640 | bytes 2211840 | tf_op jit(solution)/shard_map/psum | solution.py:126
  477.9 2.5 gather_fusion.6
  482.7 285.3 %all-reduce.3.cloned.1.call-done = f32[768,128]{0,1:T(8,128)} async-done(((f32[768,128]{0,1:T(8,128)}), f32[768,128]{0,1:T(8,128)}) %all-reduce.3.cloned.1.call-update) | async-done | bytes 393232 | tf_op jit(solution)/shard_map/psum | solution.py:142
  (365 shorter events, 125.8 us)
Async XLA Ops:
  7.2 33.7 %copy-start = (bf16[4,32,768]{2,1,0:T(8,128)(2,1)S(1)}, bf16[4,32,768]{2,1,0:T(8,128)(2,1)}, u32[]{:S(2)}) copy-start(bf16[4,32,768]{2,1,0:T(8,128)(2,1)} %param.10) | copy-start | bytes 589828
  7.2 16.0 %copy-start.4 = (bf16[48,128]{1,0:T(8,128)(2,1)S(1)}, bf16[48,128]{1,0:T(8,128)(2,1)}, u32[]{:S(2)}) copy-start(bf16[48,128]{1,0:T(8,128)(2,1)} %param.11) | copy-start | bytes 36868
  11.3 38.5 %all-to-all-start = ((s32[16,1,12]{2,1,0:T(1,128)}), s32[16,1,12]{2,1,0:T(1,128)S(1)}, u32[]{:S(2)}, u32[]{:S(2)}) async-start(s32[16,1,12]{2,1,0:T(1,128)} %bitcast.13), calls=%async_computation | async-start | bytes 16384 | tf_op jit(solution)/shard_map/all_to_all | solution.py:100
  49.9 4.9 copy-start.3
  49.9 43.4 %copy-start.1 = (s32[16]{0:T(128)S(1)}, s32[16]{0:T(128)}, u32[]{:S(2)}) copy-start(s32[16]{0:T(128)} %param.13) | copy-start | bytes 196
  49.9 43.4 %all-to-all-start.1 = ((bf16[16,12,32,128]{3,2,1,0:T(8,128)(2,1)}), bf16[16,12,32,128]{3,2,1,0:T(8,128)(2,1)}, u32[]{:S(2)}, u32[]{:S(2)}) async-start(bf16[16,12,32,128]{3,2,1,0:T(8,128)(2,1)} %bitcast.16), calls=%async_computation.1 | async-start | bytes 3145728 | tf_op jit(solution)/shard_map/all_to_all | solution.py:93
  166.1 11.2 %all-to-all-start.2 = ((f32[16,1,12]{2,1,0:T(1,128)}), f32[16,1,12]{2,1,0:T(1,128)S(1)}, u32[]{:S(2)}, u32[]{:S(2)}) async-start(f32[16,1,12]{2,1,0:T(1,128)} %bitcast.17), calls=%async_computation.2 | async-start | bytes 16384 | tf_op jit(solution)/shard_map/all_to_all | solution.py:107
  181.6 10.9 %all-to-all-start.3 = ((f32[16,1,12]{2,1,0:T(1,128)}), f32[16,1,12]{2,1,0:T(1,128)S(1)}, u32[]{:S(2)}, u32[]{:S(2)}) async-start(f32[16,1,12]{2,1,0:T(1,128)} %bitcast.18), calls=%async_computation.3 | async-start | bytes 16384 | tf_op jit(solution)/shard_map/all_to_all | solution.py:113
  335.6 4.6 copy-start.2
  335.6 142.4 %all-to-all-start.4 = ((f32[16,12,32,128]{3,2,1,0:T(8,128)}), f32[16,12,32,128]{3,2,1,0:T(8,128)}, u32[]{:S(2)}, u32[]{:S(2)}) async-start(f32[16,12,32,128]{3,2,1,0:T(8,128)} %get-tuple-element.91), calls=%async_computation.4 | async-start | bytes 6291456 | tf_op jit(solution)/shard_map/all_to_all | solution.py:119
  340.1 427.9 %all-reduce.3.cloned.1.call-start = ((), (), s32[]{:S(2)}) async-start(), calls=%async_computation.5 | async-start | bytes 786432 | tf_op jit(solution)/shard_map/psum | solution.py:142
Sparse Core Ops, SparseCore 0:
  481.9 286.0 all-reduce.2
where the time goes:
time: 780 us; the launch traced here: 777 us
  waiting for transfers between devices  337 us (43%)
  blocking collectives  154 us (20%)
  matrix products  85.5 us (11%)
  local copies, waits for them, and re-layouts  85.1 us (11%)
  other arithmetic  69.6 us (9%)
  starting transfers between devices  29.4 us (4%)
  between operations  14.2 us (2%)
    psum x1, waiting for transfers between devices, shards(): weight_total = lax.psum(weight_term, ('dp', 'passage'))  285 us
    psum x1, blocking collectives, shards(): cache_total = lax.psum(cache_accum, 'dp')  136 us
    scatter-add x16, other arithmetic, one_source(): return (accum.at[safe_slot].add(passage_tile_gradient), query_gradient)  58.2 us
    dot_general x32, matrix products, tile_scores(): jnp.einsum('cqd,cpd->cqp', query_block, passage_tiles, preferred_element_...  44.9 us
    all_to_all x1, waiting for transfers between devices, shards(): lax.all_to_all(send_queries.reshape(owners, capacity, query_len, feat_wid...  38.3 us
    dot_general x16, matrix products, one_source(): jnp.einsum('cqp,cqd->cpd', weight_halfwidth, query_block, preferred_eleme...  22.2 us
    gather x32, local copies, waits for them, and re-layouts, tile_scores(): passage_tiles = cache[safe_slot]  21.2 us
    gather x32, local copies, waits for them, and re-layouts, tile_scores(): valid = positions[None, :] < lengths[safe_slot][:, None]  21 us
  transfers between devices with their start and end apart: 6, of which 4 were waited for; matrix products, arithmetic and copies ran while one was open for 1% of the time, Pallas kernels for 0%

commit v1 on v0

v1 whole, which is shorter than its diff:
```python
import functools
import math

import jax
import jax.numpy as jnp
from jax import lax
from jax.experimental import pallas as pl
from jax.experimental.pallas import tpu as pltpu
from jax.sharding import PartitionSpec as P

TAU = 0.1
EPS = 1e-06

NX, NY, NZ, NC = 4, 8, 8, 2
OWNERS = NZ * NC
Q_DEV, QL, CAND = 4, 32, 16
PASS_DEV, PLEN, ROWS = 16, 180, 192
DIM = 128
GROUPS = 60
SLOTS = 256
ENTRIES = 192
NEG = -1e30

F32, BF16, I32 = jnp.float32, jnp.bfloat16, jnp.int32


def dot(a, b):
    return jnp.dot(a, b, preferred_element_type=F32)


def dot_nt(a, b):
    return lax.dot_general(a, b, (((1,), (1,)), ((), ())), preferred_element_type=F32)


def dot_tn(a, b):
    return lax.dot_general(a, b, (((0,), (0,)), ((), ())), preferred_element_type=F32)


def iota(shape, axis):
    return lax.broadcasted_iota(I32, shape, axis)


def ind(cond, dtype=F32):
    return jnp.where(cond, 1.0, 0.0).astype(dtype)


def pieces(x):
    a = x.astype(BF16)
    rest = x - a.astype(F32)
    b = rest.astype(BF16)
    return (a, b, (rest - b.astype(F32)).astype(BF16))


class Place:
    def __init__(self):
        self.me = lax.axis_index("passage")
        self.z, self.c = self.me // NC, lax.rem(self.me, NC)
        self.sibling = self.z * NC + (1 - self.c)

    def ring(self, k):
        return lax.rem(self.z + k, NZ) * NC + self.c

    def ring_sibling(self, k):
        return lax.rem(self.z + k, NZ) * NC + (1 - self.c)


def remote(src, dst, send, recv, device):
    return pltpu.make_async_remote_copy(
        src_ref=src,
        dst_ref=dst,
        send_sem=send,
        recv_sem=recv,
        device_id=device,
        device_id_type=pl.DeviceIdType.MESH,
    )


def greet(devices):
    barrier = pltpu.get_barrier_semaphore()
    for device in devices:
        pl.semaphore_signal(
            barrier, inc=1, device_id=device, device_id_type=pl.DeviceIdType.MESH
        )
    pl.semaphore_wait(barrier, len(devices))


NEAR = (1, 7, 2, 6, 3, 5, 4)


class Gather:
    def __init__(self, place, buf, send, recv):
        self.place, self.buf, self.send, self.recv = place, buf, send, recv
        self.sent = []

    def copy(self, slot, n, peer):
        return remote(
            self.buf.at[slot], self.buf.at[slot], self.send.at[n], self.recv.at[slot],
            {"passage": peer},
        )

    def start(self):
        p = self.place
        for n, k in enumerate(NEAR):
            self.sent.append(self.copy(p.me, n, p.ring(k)))
            self.sent[-1].start()
        self.sent.append(self.copy(p.me, NZ - 1, p.sibling))
        self.sent[-1].start()

    def finish(self):
        p = self.place
        for n, k in enumerate(NEAR):
            forward = self.copy(p.ring(k), NZ + n, p.sibling)
            forward.wait_recv()
            forward.start()
            self.sent.append(forward)
        self.copy(p.sibling, 0, p.sibling).wait_recv()
        for k in NEAR:
            self.copy(p.ring_sibling(k), 0, p.sibling).wait_recv()
        for copy in self.sent:
            copy.wait_send()


def gather_sems():
    return [pltpu.SemaphoreType.DMA((2 * NZ - 1,)), pltpu.SemaphoreType.DMA((OWNERS,))]


def routing_tables(rows, me, tab_ref, hit_ref):
    rows_t = dot_nt(ind(iota((CAND, 128), 0) == iota((CAND, 128), 1), BF16), rows.astype(BF16))
    local = rows_t - (PASS_DEV * me).astype(F32)
    own = ind((local >= 0) & (local < PASS_DEV))
    hit = jnp.concatenate([ind(local == r) for r in range(PASS_DEV)], axis=0)
    lane_i, lane_j = iota((128, 128), 0), iota((128, 128), 1)
    upto = ind(lane_i <= lane_j, BF16)
    before = ind(lane_i < lane_j, BF16)
    ones = jnp.ones((128, 128), BF16)
    hit_bf = hit.astype(BF16)
    seen = dot(hit_bf, upto)
    total = dot(hit_bf, ones).astype(BF16)
    big_i, big_j = iota((256, 256), 0), iota((256, 256), 1)
    row_i, row_j = big_i // CAND, big_j // CAND
    ahead = dot(ind((row_i == row_j) & (big_j < big_i), BF16), total)
    number = dot(ind(row_i == row_j, BF16), total)
    groups = jnp.floor((number + 3.0) * 0.25)
    first = dot(
        ind((row_j < row_i) & (big_j == row_j * CAND), BF16), groups.astype(BF16)
    )
    rank = seen - 1.0 + ahead
    lap = jnp.floor(rank * 0.25)
    spot = 64.0 * (rank - 4.0 * lap) + first + lap
    place4 = 4.0 * (first + lap) + (rank - 4.0 * lap)

    def pick(values):
        out = jnp.zeros((CAND, 128), F32)
        for r in range(PASS_DEV):
            part = slice(r * CAND, (r + 1) * CAND)
            out = out + hit[part] * values[part]
        return out

    slot = jnp.where(own > 0, pick(spot), -1.0)
    place4 = pick(place4)
    cand = iota((CAND, 128), 0).astype(F32)
    code = CAND * cand + jnp.where(own > 0, local, 0.0)

    own_bf = own.astype(BF16)
    c_i, c_j = iota((CAND, CAND), 0), iota((CAND, CAND), 1)
    count = dot(jnp.ones((CAND, CAND), BF16), own_bf)
    earlier = dot(count.astype(BF16), before)
    entry = earlier + dot(ind(c_j < c_i, BF16), own_bf)
    entry = jnp.where(own > 0, entry, -1.0)
    last_entry = jnp.where(count > 0, earlier + count - 1.0, -1.0)

    lane = iota((8, 128), 1)
    query = ((lane // 8) * Q_DEV + lax.rem(lane, 8)).astype(F32).astype(BF16)
    one8 = jnp.ones((8, 128), BF16)
    qn, codes, valid, entry_place, entry_q = [], [], [], [], []
    for j in range(4):
        at = (iota((64, 128), 0) + 64 * j).astype(F32)
        acc = [jnp.zeros((64, 128), F32) for _ in range(4)]
        for c in range(CAND):
            one = ind(at == slot[c : c + 1])
            acc[0] = acc[0] + one
            acc[1] = acc[1] + one * code[c : c + 1]
            one = ind(at == entry[c : c + 1])
            acc[2] = acc[2] + one * place4[c : c + 1]
            acc[3] = acc[3] + one
        acc = [a.astype(BF16) for a in acc]
        hit_ref[64 * j : 64 * j + 64] = acc[0]
        qn.append(acc[0])
        codes.append(acc[1])
        entry_place.append(acc[2])
        entry_q.append(acc[3])
    at_slot = jnp.concatenate(qn, axis=0)
    qn = dot_nt(query, at_slot)
    valid = dot_nt(one8, at_slot)
    codes = dot_nt(one8, jnp.concatenate(codes, axis=0))
    entry_place = dot_nt(one8, jnp.concatenate(entry_place, axis=0))
    entry_q = dot_nt(query, jnp.concatenate(entry_q, axis=0))
    cands = jnp.floor(codes / CAND)
    row_of = codes - CAND * cands
    cands = jnp.where(valid > 0, cands, -1.0)

    last_group = jnp.where(number > 0, first + groups, 0.0)
    big = iota((256, 128), 0)
    diag = (big == iota((256, 128), 1) * CAND) & (iota((256, 128), 1) < PASS_DEV)
    last_row = dot(jnp.ones((8, 256), BF16), jnp.where(diag, last_group, 0.0).astype(BF16)) - 1.0
    pad = jnp.zeros((8, 128), F32)
    last_row = jnp.concatenate([last_row, pad], axis=1)
    last_entry = jnp.concatenate([last_entry[:8], pad], axis=1)

    sub = iota((8, SLOTS), 0)
    table = jnp.zeros((8, SLOTS), F32)
    rows_of_table = (qn, row_of, entry_place, entry_q, last_row, last_entry, cands)
    for n, values in enumerate(rows_of_table):
        table = jnp.where(sub == n, values, table)
    tab_ref[...] = table.astype(I32)


def gather_kernel(
    hidden_ref, weight_ref, ids_ref, map_ref,
    query_ref, full_ref, raw_ref, tab_ref, hit_ref,
    rows_buf, w_send, w_recv, r_send, r_recv, q_send, q_recv,
):
    place = Place()
    me = place.me
    full_ref[me] = weight_ref[...]
    near = [{"passage": place.ring(k)} for k in NEAR] + [{"passage": place.sibling}]
    greet(near)
    weights = Gather(place, full_ref, w_send, w_recv)
    weights.start()

    table = jnp.broadcast_to(map_ref[...].astype(F32), (8, 256)).astype(BF16)
    own = jnp.full((8, CAND), -1.0, F32)
    for q in range(Q_DEV):
        one = ind(iota((256, CAND), 0) == ids_ref[q : q + 1, :], BF16)
        own = jnp.where(iota((8, CAND), 0) == q, dot(table, one), own)
    rows_buf[me] = jnp.full((8, 128), -1.0, F32)
    rows_buf[me, :, 0:CAND] = own
    rows = Gather(place, rows_buf, r_send, r_recv)
    rows.start()

    weights.finish()
    raw = dot(hidden_ref[...], full_ref[...].reshape(-1, DIM))
    raw_ref[...] = raw
    inverse = lax.rsqrt(jnp.mean(raw * raw, axis=-1, keepdims=True) + EPS)
    query_ref[me] = (raw * inverse).astype(BF16)
    queries = Gather(place, query_ref, q_send, q_recv)
    queries.start()

    rows.finish()
    routing_tables(rows_buf[...].reshape(OWNERS * 8, 128), me, tab_ref, hit_ref)
    queries.finish()


def owner_kernel(
    cache_ref, len_ref, tab, tab_vec, hit_ref, query_ref,
    cg_ref, qg_ref,
    tiles, exps, logs, recips, scales, cg_run, qg_group, qg_run, score_buf, s_send, s_recv,
):
    place = Place()
    me = place.me
    others = [lax.rem(me + k, OWNERS) for k in range(1, OWNERS)]
    similarity_scale = 1.0 / (TAU * math.sqrt(DIM))
    root_scale = 1.0 / math.sqrt(DIM)

    for r in range(PASS_DEV):
        tiles[r, ROWS - 16 : ROWS] = jnp.zeros((16, DIM), BF16)
        tiles[r, 0:PLEN] = cache_ref[r]
    logs[...] = jnp.zeros_like(logs)
    recips[...] = jnp.zeros_like(recips)

    def load_queries(g):
        return jnp.concatenate([query_ref[tab[0, 64 * j + g]] for j in range(4)], axis=0)

    live = iota((ROWS, 128), 0)

    def forward(i, _):
        for u in range(4):
            g = 4 * i + u
            row = tab[1, g]
            sims = dot_nt(tiles[row], load_queries(g)) * similarity_scale
            sims = jnp.where(live < len_ref[row], sims, NEG)
            top = jnp.max(sims, axis=0, keepdims=True)
            e = jnp.exp(sims - top)
            total = jnp.sum(e, axis=0, keepdims=True)
            exps[g] = e
            logs[pl.ds(g, 1), :] = top + jnp.log(total)
            recips[pl.ds(g, 1), :] = 1.0 / total
        return 0

    lax.fori_loop(0, GROUPS // 4, forward, 0)

    of_place = iota((SLOTS, 128), 1) // QL == iota((SLOTS, 128), 0) // 64
    spread = jnp.where(of_place, jnp.concatenate([logs[...]] * 4, axis=0), 0.0)
    one8 = jnp.ones((8, 128), BF16)
    score_row = TAU * sum(dot_nt(one8, part) for part in pieces(spread))
    cands = tab_vec[6:7, :]
    is_cand = ind(iota((CAND, SLOTS), 0) == cands)
    hits = hit_ref[...]
    mine = sum(
        dot((is_cand * part[0:1].astype(F32)).astype(BF16), hits) for part in pieces(score_row)
    )
    score_buf[me] = mine[0:8] + pltpu.roll(mine[8:16], 4, 1)

    greet([{"passage": d} for d in others])
    copies = []
    for n, d in enumerate(others):
        copies.append(
            remote(score_buf.at[me], score_buf.at[me], s_send.at[n], s_recv.at[me], {"passage": d})
        )
        copies[-1].start()
    for d in others:
        remote(score_buf.at[d], score_buf.at[d], s_send.at[0], s_recv.at[d], {"passage": d}).wait_recv()
    for copy in copies:
        copy.wait_send()
    scores = score_buf[0]
    for d in range(1, OWNERS):
        scores = scores + score_buf[d]

    lane = iota((8, 128), 1)
    low = lax.rem(lane, 8) < Q_DEV

    def both(x, op):
        return op(x, jnp.where(low, pltpu.roll(x, 124, 1), pltpu.roll(x, 4, 1)))

    top = both(jnp.broadcast_to(jnp.max(scores, axis=0, keepdims=True), (8, 128)), jnp.maximum)
    e = jnp.exp(scores - top)
    total = both(jnp.broadcast_to(jnp.sum(e, axis=0, keepdims=True), (8, 128)), jnp.add)
    grad = e / total - ind((iota((8, 128), 0) == 0) & low)
    grad = jnp.concatenate(
        [jnp.where(low, grad, 0.0), jnp.where(low, pltpu.roll(grad, 124, 1), 0.0)], axis=0
    )
    at_slot = is_cand * sum(dot_nt(part, hits) for part in pieces(grad))
    at_slot = jnp.sum(at_slot, axis=0, keepdims=True)
    same_group = ind(lax.rem(iota((64, SLOTS), 1), 64) == iota((64, SLOTS), 0))
    to_lanes = ind(of_place, BF16)
    by_lane = sum(dot(part, to_lanes) for part in pieces(same_group * at_slot))
    scales[...] = by_lane * recips[...] * root_scale

    def backward(i, _):
        for u in range(4):
            g = 4 * i + u
            row = tab[1, g]
            w = (exps[g] * scales[pl.ds(g, 1), :]).astype(BF16)
            again = (row == tab[1, jnp.maximum(g - 1, 0)]) & (g > 0)
            cg_run[g + 1] = jnp.where(again, cg_run[g], 0.0) + dot(w, load_queries(g))
            qg_group[g] = dot_tn(w, tiles[row]).reshape(4, QL, DIM)
        return 0

    lax.fori_loop(0, GROUPS // 4, backward, 0)

    def finish_row(r, _):
        last = tab[4, r]
        cg_ref[r] = jnp.where(last >= 0, cg_run[jnp.maximum(last, 0) + 1], 0.0).astype(BF16)
        return 0

    lax.fori_loop(0, PASS_DEV, finish_row, 0)

    def entry_step(i, _):
        for u in range(4):
            e = 4 * i + u
            at = tab[2, e]
            again = (tab[3, e] == tab[3, jnp.maximum(e - 1, 0)]) & (e > 0)
            part = qg_group[at // 4, lax.rem(at, 4)]
            qg_run[e + 1] = jnp.where(again, qg_run[e], 0.0) + part
        return 0

    lax.fori_loop(0, ENTRIES // 4, entry_step, 0)

    def finish_query(q, _):
        last = tab[5, (q // Q_DEV) * 8 + lax.rem(q, Q_DEV)]
        qg_ref[q] = jnp.where(last >= 0, qg_run[jnp.maximum(last, 0) + 1], 0.0).astype(BF16)
        return 0

    lax.fori_loop(0, OWNERS * Q_DEV, finish_query, 0)


class Ring:
    def __init__(self, n, at, device, rows, cut, send, recv):
        self.n, self.at, self.device = n, at, device
        self.rows, self.cut, self.half = rows, cut, n // 2
        self.send, self.recv = send, recv

    def peer(self, k):
        return lax.rem(self.at + k + self.n, self.n)

    def span(self, base, t, part=None):
        lo, hi = 0, self.rows
        if part == 0:
            hi = self.cut
        if part == 1:
            lo = self.cut
        return pl.ds(pl.multiple_of(base + t * self.rows + lo, 16), hi - lo)

    def copy(self, src, dst, way, step):
        toward = self.device(self.peer(1 if way == 0 else -1))
        return remote(src, dst, self.send.at[way, step - 1], self.recv.at[way, step - 1], toward)


class Scatter(Ring):
    def bind(self, src, base, arrive):
        self.src, self.base, self.arrive = src, base, arrive
        return self

    def part(self, way):
        return slice(0, self.cut) if way == 0 else slice(self.cut, self.rows)

    def make(self, step, way):
        if step == 1:
            t = self.peer(self.half)
            src = self.src.at[self.span(self.base, t, way), :]
            dst = self.arrive.at[way, 0, self.part(way)]
        else:
            src = self.arrive.at[way, step - 2]
            dst = self.arrive.at[way, step - 1]
        return self.copy(src, dst, way, step)

    def start(self, step):
        for way in (0, 1):
            self.make(step, way).start()

    def finish(self, step):
        for way in (0, 1):
            self.make(step, way).wait_recv()
            if step == self.half:
                continue
            t = self.peer((self.half - step) * (1 if way == 0 else -1))
            own = self.src[self.span(self.base, t), :]
            if step == 1:
                part = self.part(way)
                for rows in (slice(0, self.cut), slice(self.cut, self.rows)):
                    mine = own[rows]
                    if rows == part:
                        mine = (mine.astype(F32) + self.arrive[way, 0, rows].astype(F32)).astype(BF16)
                    if step > 1 or rows != part:
                        self.arrive[way, 0, rows] = mine
                    else:
                        self.arrive[way, 0, rows] = mine
            else:
                both = own.astype(F32) + self.arrive[way, step - 1].astype(F32)
                self.arrive[way, step - 1] = both.astype(BF16)

    def result(self):
        own = self.src[self.span(self.base, self.at), :].astype(F32)
        return own + self.arrive[0, self.half - 1].astype(F32) + self.arrive[1, self.half - 1].astype(F32)

    def drain(self):
        for step in range(1, self.half + 1):
            for way in (0, 1):
                self.make(step, way).wait_send()


class Spread(Ring):
    def bind(self, buf, base):
        self.buf, self.base = buf, base
        return self

    def make(self, step, way, arriving=False):
        t = self.peer((step if arriving else step - 1) * (-1 if way == 0 else 1))
        span = self.span(self.base, t, way if step == self.half else None)
        return self.copy(self.buf.at[span, :], self.buf.at[span, :], way, step)

    def start(self, step):
        for way in (0, 1):
            self.make(step, way).start()

    def finish(self, step):
        for way in (0, 1):
            self.make(step, way, arriving=True).wait_recv()

    def drain(self):
        for step in range(1, self.half + 1):
            for way in (0, 1):
                self.make(step, way).wait_send()


class Swap:
    def __init__(self, n, at, device, send, recv):
        self.n, self.at, self.device, self.send, self.recv = n, at, device, send, recv

    def start(self, src_of, buf):
        self.buf, self.copies = buf, []
        for k in range(1, self.n):
            t = lax.rem(self.at + k, self.n)
            copy = remote(
                src_of(t), buf.at[self.at], self.send.at[k - 1], self.recv.at[self.at], self.device(t)
            )
            copy.start()
            self.copies.append(copy)

    def finish(self):
        for k in range(1, self.n):
            t = lax.rem(self.at + k, self.n)
            remote(
                self.buf.at[t], self.buf.at[t], self.send.at[0], self.recv.at[t], self.device(t)
            ).wait_recv()

    def drain(self):
        for copy in self.copies:
            copy.wait_send()


HALF_ROWS = PASS_DEV * ROWS // 2
AX, BY = HALF_ROWS // NX, HALF_ROWS // NY
SUB = HALF_ROWS // (NX * NY)


def sum_kernel(
    cg_ref, qg_ref, hidden_ref, full_ref, raw_ref,
    hid_ref, wg_ref, cache_ref,
    ax_buf, ay_buf, by_buf, bx_buf, mid_a, mid_b, fin, q_sib, q_out, q_in,
    w_own, w_sib, w_out, w_in, w_x, w_y,
    *sems,
):
    place = Place()
    me, z, c = place.me, place.z, place.c
    dp = lax.axis_index("dp")
    ix, iy = dp // NY, lax.rem(dp, NY)
    sems = list(sems)

    def take():
        return sems.pop(0), sems.pop(0)

    on_x = lambda t: {"dp": t * NY + iy}
    on_y = lambda t: {"dp": ix * NY + t}
    on_z = lambda t: {"passage": t * NC + c}
    sibling = {"passage": place.sibling}
    greet(
        [sibling]
        + [on_z(lax.rem(z + k, NZ)) for k in range(1, NZ)]
        + [on_x(lax.rem(ix + k, NX)) for k in range(1, NX)]
        + [on_y(lax.rem(iy + k, NY)) for k in range(1, NY)]
    )

    a1 = Scatter(NX, ix, on_x, AX, AX // 2, *take()).bind(cg_ref, 0, ax_buf)
    b1 = Scatter(NY, iy, on_y, BY, BY // 2, *take()).bind(cg_ref, HALF_ROWS, by_buf)
    a2 = Scatter(NY, iy, on_y, SUB, 32, *take()).bind(mid_a, 0, ay_buf)
    b2 = Scatter(NX, ix, on_x, SUB, 32, *take()).bind(mid_b, 0, bx_buf)
    a3 = Spread(NY, iy, on_y, SUB, 32, *take()).bind(fin, ix * AX)
    b3 = Spread(NX, ix, on_x, SUB, 32, *take()).bind(fin, HALF_ROWS + iy * BY)
    a4 = Spread(NX, ix, on_x, AX, AX // 2, *take()).bind(fin, 0)
    b4 = Spread(NY, iy, on_y, BY, BY // 2, *take()).bind(fin, HALF_ROWS)
    q_swap = Swap(NZ, z, on_z, *take())
    w_swap = Swap(NZ, z, on_z, *take())
    x_swap = Swap(NX, ix, on_x, *take())
    y_swap = Swap(NY, iy, on_y, *take())
    qs_send, qs_recv = take()
    ws_send, ws_recv = take()

    q_pair = remote(qg_ref.at[:, 1 - c], q_sib, qs_send, qs_recv, sibling)
    q_pair.start()
    a1.start(1)
    b1.start(1)
    q_pair.wait_recv()
    for t in range(NZ):
        q_out[t] = (qg_ref[t, c].astype(F32) + q_sib[t].astype(F32)).astype(BF16)
    q_swap.start(lambda t: q_out.at[t], q_in)

    a1.finish(1)
    a1.start(2)
    b1.finish(1)
    b1.start(2)
    b1.finish(2)
    b1.start(3)
    a1.finish(2)
    mid_a[...] = a1.result().astype(BF16)
    a2.start(1)
    b1.finish(3)
    b1.start(4)

    q_swap.finish()
    query_gradient = q_out[z].astype(F32)
    for k in range(1, NZ):
        query_gradient = query_gradient + q_in[lax.rem(z + k, NZ)].astype(F32)
    raw = raw_ref[...]
    inverse = lax.rsqrt(jnp.mean(raw * raw, axis=-1, keepdims=True) + EPS)
    mean_term = jnp.mean(query_gradient * raw, axis=-1, keepdims=True)
    raw_grad = (
        inverse * query_gradient - raw * (inverse * inverse * inverse) * mean_term
    ).astype(BF16)
    weight_part = dot_tn(hidden_ref[...], raw_grad)
    w_own[...] = weight_part.astype(BF16).reshape(w_own.shape)
    w_pair = remote(w_own.at[:, 1 - c], w_sib, ws_send, ws_recv, sibling)
    w_pair.start()

    a2.finish(1)
    a2.start(2)
    b1.finish(4)
    mid_b[...] = b1.result().astype(BF16)
    b2.start(1)
    hid_ref[...] = dot_nt(raw_grad, full_ref[...].reshape(-1, DIM)).astype(BF16)
    w_pair.wait_recv()
    for t in range(NZ):
        w_out[t] = (w_own[t, c].astype(F32) + w_sib[t].astype(F32)).astype(BF16)
    w_swap.start(lambda t: w_out.at[t], w_in)

    a2.finish(2)
    a2.start(3)
    b2.finish(1)
    b2.start(2)
    a2.finish(3)
    a2.start(4)
    b2.finish(2)
    fin[b3.span(b3.base, ix), :] = b2.result().astype(BF16)
    b3.start(1)
    a2.finish(4)
    fin[a3.span(a3.base, iy), :] = a2.result().astype(BF16)
    a3.start(1)

    w_swap.finish()
    total = w_out[z].astype(F32)
    for k in range(1, NZ):
        total = total + w_in[lax.rem(z + k, NZ)].astype(F32)
    w_x[ix] = total.astype(BF16)
    x_swap.start(lambda t: w_x.at[ix], w_x)

    b3.finish(1)
    b3.start(2)
    a3.finish(1)
    a3.start(2)
    b3.finish(2)
    b4.start(1)
    a3.finish(2)
    a3.start(3)
    b4.finish(1)
    b4.start(2)

    x_swap.finish()
    total = w_x[0].astype(F32)
    for t in range(1, NX):
        total = total + w_x[t].astype(F32)
    w_y[iy] = total.astype(BF16)
    y_swap.start(lambda t: w_y.at[iy], w_y)

    a3.finish(3)
    a3.start(4)
    b4.finish(2)
    b4.start(3)
    a3.finish(4)
    a4.start(1)
    b4.finish(3)
    b4.start(4)
    a4.finish(1)
    a4.start(2)

    y_swap.finish()
    total = w_y[0].astype(F32)
    for t in range(1, NY):
        total = total + w_y[t].astype(F32)
    wg_ref[...] = total

    b4.finish(4)
    for r in range(PASS_DEV // 2, PASS_DEV):
        cache_ref[r] = fin[r * ROWS : (r + 1) * ROWS, :][0:PLEN]
    a4.finish(2)
    for r in range(PASS_DEV // 2):
        cache_ref[r] = fin[r * ROWS : (r + 1) * ROWS, :][0:PLEN]

    q_pair.wait_send()
    w_pair.wait_send()
    for moved in (a1, b1, a2, b2, a3, b3, a4, b4, q_swap, w_swap, x_swap, y_swap):
        moved.drain()


def call(kernel, collective_id, out_shape, in_specs, scratch, args):
    return pl.pallas_call(
        kernel,
        out_shape=out_shape,
        in_specs=in_specs,
        out_specs=[VMEM] * len(out_shape),
        scratch_shapes=scratch,
        compiler_params=pltpu.CompilerParams(
            collective_id=collective_id, has_side_effects=True, vmem_limit_bytes=56 * 2**20
        ),
    )(*args)


VMEM = pl.BlockSpec(memory_space=pltpu.VMEM)
SMEM = pl.BlockSpec(memory_space=pltpu.SMEM)


def shards(hidden, weight, cache, lengths, passage_ids, owner_map):
    width = hidden.shape[-1]
    share = width // OWNERS
    tokens = Q_DEV * QL
    shape = jax.ShapeDtypeStruct
    dma = pltpu.SemaphoreType.DMA
    hidden = hidden.reshape(tokens, width)
    queries, full, raw, tab, hits = call(
        gather_kernel,
        0,
        [
            shape((OWNERS, tokens, DIM), BF16),
            shape((OWNERS, share, DIM), BF16),
            shape((tokens, DIM), F32),
            shape((8, SLOTS), I32),
            shape((SLOTS, 128), BF16),
        ],
        [VMEM] * 4,
        [pltpu.VMEM((OWNERS, 8, 128), F32)] + gather_sems() + gather_sems() + gather_sems(),
        (hidden, weight, passage_ids, owner_map.reshape(1, -1)),
    )
    cg, qg = call(
        owner_kernel,
        1,
        [
            shape((PASS_DEV, ROWS, DIM), BF16),
            shape((OWNERS * Q_DEV, QL, DIM), BF16),
        ],
        [VMEM, SMEM, SMEM, VMEM, VMEM, VMEM],
        [
            pltpu.VMEM((PASS_DEV, ROWS, DIM), BF16),
            pltpu.VMEM((GROUPS, ROWS, 128), F32),
            pltpu.VMEM((64, 128), F32),
            pltpu.VMEM((64, 128), F32),
            pltpu.VMEM((64, 128), F32),
            pltpu.VMEM((GROUPS + 1, ROWS, DIM), F32),
            pltpu.VMEM((GROUPS, 4, QL, DIM), F32),
            pltpu.VMEM((ENTRIES + 1, QL, DIM), F32),
            pltpu.VMEM((OWNERS, 8, 128), F32),
            dma((OWNERS - 1,)),
            dma((OWNERS,)),
        ],
        (cache, lengths, tab, tab, hits, queries.reshape(OWNERS * Q_DEV, QL, DIM)),
    )

    def ring(n):
        return [dma((2, n // 2)), dma((2, n // 2))]

    def swap(n):
        return [dma((n - 1,)), dma((n,))]

    sems = ring(NX) + ring(NY) + ring(NY) + ring(NX) + ring(NY) + ring(NX) + ring(NX) + ring(NY)
    sems += swap(NZ) + swap(NZ) + swap(NX) + swap(NY) + [dma, dma, dma, dma]
    hid, wg, cache_grad = call(
        sum_kernel,
        2,
        [
            shape((tokens, width), BF16),
            shape((share, DIM), F32),
            shape((PASS_DEV, PLEN, DIM), BF16),
        ],
        [VMEM] * 5,
        [
            pltpu.VMEM((2, NX // 2, AX, DIM), BF16),
            pltpu.VMEM((2, NY // 2, SUB, DIM), BF16),
            pltpu.VMEM((2, NY // 2, BY, DIM), BF16),
            pltpu.VMEM((2, NX // 2, SUB, DIM), BF16),
            pltpu.VMEM((AX, DIM), BF16),
            pltpu.VMEM((BY, DIM), BF16),
            pltpu.VMEM((PASS_DEV * ROWS, DIM), BF16),
            pltpu.VMEM((NZ, tokens, DIM), BF16),
            pltpu.VMEM((NZ, tokens, DIM), BF16),
            pltpu.VMEM((NZ, tokens, DIM), BF16),
            pltpu.VMEM((NZ, NC, share, DIM), BF16),
            pltpu.VMEM((NZ, share, DIM), BF16),
            pltpu.VMEM((NZ, share, DIM), BF16),
            pltpu.VMEM((NZ, share, DIM), BF16),
            pltpu.VMEM((NX, share, DIM), BF16),
            pltpu.VMEM((NY, share, DIM), BF16),
        ]
        + sems,
        (
            cg.reshape(PASS_DEV * ROWS, DIM),
            qg.reshape(NZ, NC, tokens, DIM),
            hidden,
            full,
            raw,
        ),
    )
    return hid.reshape(Q_DEV, QL, width), wg, cache_grad


def solution(mesh):
    in_specs = (
        P(("dp", "passage"), None, None),
        P("passage", None),
        P("passage", None, None),
        P("passage"),
        P(("dp", "passage"), None),
        P(),
    )
    out_specs = (P(("dp", "passage"), None, None), P("passage", None), P("passage", None, None))
    return jax.shard_map(shards, mesh=mesh, in_specs=in_specs, out_specs=out_specs, check_vma=False)
```

time: 780 us -> 118 us (0.15)
  the two profiles are of different devices: /device:TPU:1 before, /device:TPU:8 now
where the time goes in v1:
time: 118 us; the launch traced here: 117 us
  Pallas kernels  111 us (94%)
  local copies, waits for them, and re-layouts  5.66 us (5%)
    pallas_call x3, Pallas kernels, call(): pl.pallas_call(kernel, out_shape=out_shape, in_specs=in_specs, out_specs=...  111 us
    unnamed x8, local copies, waits for them, and re-layouts  5.66 us

profile of v1, /device:TPU:8, one launch (start us, length us, event | category | flops | bytes accessed | tf_op | source)
XLA Modules:
  0.0 117.3 jit_solution(1734883168671544120)
XLA Ops:
  0.6 2.2 %copy.9.cache_ref = bf16[16,180,128]{2,1,0:T(8,128)(2,1)} copy(bf16[16,180,128]{2,0,1:T(8,128)(2,1)} %param.8) | data formatting | bytes 1474560 | tf_op args[2]
  2.8 29.7 %shard_map.85 = (bf16[16,128,128]{2,1,0:T(8,128)(2,1)}, bf16[16,48,128]{2,1,0:T(8,128)(2,1)}, f32[128,128]{1,0:T(8,128)}, s32[8,256]{1,0:T(8,128)}, bf16[256,128]{1,0:T(8,128)(2,1)}) custom-call(bf16[128,768]{1,0:T(8,128)(2,1)} %bitcast.7, bf16[48,128]{1,0:T(8,128)(2,1)} %weight_ref.1, s32[4,16]{1,0:T(4,128)} %ids_ref.1, s32[1,256]{1,0:T(1,128)} %bitcast.12), custom_call_target="tpu_custom_call" | custom-call | tf_op jit(solution)/shard_map/pallas_call | solution.py:665
  32.5 26.2 %shard_map.86 = (bf16[16,192,128]{2,1,0:T(8,128)(2,1)}, bf16[64,32,128]{2,1,0:T(8,128)(2,1)}) custom-call(bf16[16,180,128]{2,1,0:T(8,128)(2,1)} %copy.9.cache_ref, s32[16]{0:T(128)} %len_ref.1, s32[8,256]{1,0:T(8,128)} %get-tuple-element.13.tab.tab_vec, s32[8,256]{1,0:T(8,128)} %get-tuple-element.13.tab.tab_vec, bf16[256,128]{1,0:T(8,128)(2,1)} %get-tuple-element.14.hit_ref, ...), custom_call_target="tpu_custom_call" | custom-call | tf_op jit(solution)/shard_map/pallas_call | solution.py:665
  58.7 55.1 %shard_map.87 = (bf16[128,768]{1,0:T(8,128)(2,1)}, f32[48,128]{1,0:T(8,128)}, bf16[16,180,128]{2,1,0:T(8,128)(2,1)}) custom-call(bf16[3072,128]{1,0:T(8,128)(2,1)} %bitcast.6, bf16[8,2,128,128]{3,2,1,0:T(8,128)(2,1)} %bitcast.9, bf16[128,768]{1,0:T(8,128)(2,1)} %bitcast.8, bf16[16,48,128]{2,1,0:T(8,128)(2,1)} %get-tuple-element.18.full_ref, ...), custom_call_target="tpu_custom_call" | custom-call | tf_op jit(solution)/shard_map/pallas_call | solution.py:665
  113.8 0.0 copy-start
  113.8 2.1 %copy.10 = bf16[16,180,128]{2,0,1:T(8,128)(2,1)} copy(bf16[16,180,128]{2,1,0:T(8,128)(2,1)} %get-tuple-element.25) | data formatting | bytes 1474560
  115.9 0.0 copy-done
  115.9 0.0 copy-start.1
  115.9 0.7 copy.13
  116.6 0.1 copy-done.1
  116.7 0.6 copy.14
Async XLA Ops:
  113.8 2.1 %copy-start = (bf16[128,768]{1,0:T(8,128)(2,1)S(1)}, bf16[128,768]{1,0:T(8,128)(2,1)}, u32[]{:S(2)}) copy-start(bf16[128,768]{1,0:T(8,128)(2,1)} %get-tuple-element.20) | copy-start | bytes 589828
  115.9 0.7 copy-start.1

commit v2 on v1

v2 whole, which is shorter than its diff:
```python
import functools
import math

import jax
import jax.numpy as jnp
from jax import lax
from jax.experimental import pallas as pl
from jax.experimental.pallas import tpu as pltpu
from jax.sharding import PartitionSpec as P

TAU = 0.1
EPS = 1e-06

NX, NY, NZ, NC = 4, 8, 8, 2
OWNERS = NZ * NC
Q_DEV, QL, CAND = 4, 32, 16
PASS_DEV, PLEN, ROWS = 16, 180, 192
DIM = 128
GROUPS = 60
SLOTS = 256
ENTRIES = 192
NEG = -1e30

F32, BF16, I32 = jnp.float32, jnp.bfloat16, jnp.int32


def dot(a, b):
    return jnp.dot(a, b, preferred_element_type=F32)


def dot_nt(a, b):
    return lax.dot_general(a, b, (((1,), (1,)), ((), ())), preferred_element_type=F32)


def dot_tn(a, b):
    return lax.dot_general(a, b, (((0,), (0,)), ((), ())), preferred_element_type=F32)


def iota(shape, axis):
    return lax.broadcasted_iota(I32, shape, axis)


def ind(cond, dtype=F32):
    return jnp.where(cond, 1.0, 0.0).astype(dtype)


def pieces(x):
    a = x.astype(BF16)
    rest = x - a.astype(F32)
    b = rest.astype(BF16)
    return (a, b, (rest - b.astype(F32)).astype(BF16))


class Place:
    def __init__(self):
        self.me = lax.axis_index("passage")
        self.z, self.c = self.me // NC, lax.rem(self.me, NC)
        self.sibling = self.z * NC + (1 - self.c)

    def ring(self, k):
        return lax.rem(self.z + k, NZ) * NC + self.c

    def ring_sibling(self, k):
        return lax.rem(self.z + k, NZ) * NC + (1 - self.c)


def remote(src, dst, send, recv, device):
    return pltpu.make_async_remote_copy(
        src_ref=src,
        dst_ref=dst,
        send_sem=send,
        recv_sem=recv,
        device_id=device,
        device_id_type=pl.DeviceIdType.MESH,
    )


NEAR = (1, 7, 2, 6, 3, 5, 4)


class Gather:
    def __init__(self, place, buf, send, recv):
        self.place, self.buf, self.send, self.recv = place, buf, send, recv
        self.sent = []

    def copy(self, slot, n, peer):
        return remote(
            self.buf.at[slot], self.buf.at[slot], self.send.at[n], self.recv.at[slot],
            {"passage": peer},
        )

    def start(self):
        p = self.place
        for n, k in enumerate(NEAR):
            self.sent.append(self.copy(p.me, n, p.ring(k)))
            self.sent[-1].start()
        self.sent.append(self.copy(p.me, NZ - 1, p.sibling))
        self.sent[-1].start()

    def finish(self):
        p = self.place
        for n, k in enumerate(NEAR):
            forward = self.copy(p.ring(k), NZ + n, p.sibling)
            forward.wait_recv()
            forward.start()
            self.sent.append(forward)
        self.copy(p.sibling, 0, p.sibling).wait_recv()
        for k in NEAR:
            self.copy(p.ring_sibling(k), 0, p.sibling).wait_recv()
        for copy in self.sent:
            copy.wait_send()


def routing_tables(rows, me, tab_ref, hit_ref):
    rows_t = dot_nt(ind(iota((CAND, 128), 0) == iota((CAND, 128), 1), BF16), rows.astype(BF16))
    local = rows_t - (PASS_DEV * me).astype(F32)
    own = ind((local >= 0) & (local < PASS_DEV))
    hit = jnp.concatenate([ind(local == r) for r in range(PASS_DEV)], axis=0)
    lane_i, lane_j = iota((128, 128), 0), iota((128, 128), 1)
    upto = ind(lane_i <= lane_j, BF16)
    before = ind(lane_i < lane_j, BF16)
    ones = jnp.ones((128, 128), BF16)
    hit_bf = hit.astype(BF16)
    seen = dot(hit_bf, upto)
    total = dot(hit_bf, ones).astype(BF16)
    big_i, big_j = iota((256, 256), 0), iota((256, 256), 1)
    row_i, row_j = big_i // CAND, big_j // CAND
    ahead = dot(ind((row_i == row_j) & (big_j < big_i), BF16), total)
    number = dot(ind(row_i == row_j, BF16), total)
    groups = jnp.floor((number + 3.0) * 0.25)
    first = dot(
        ind((row_j < row_i) & (big_j == row_j * CAND), BF16), groups.astype(BF16)
    )
    rank = seen - 1.0 + ahead
    lap = jnp.floor(rank * 0.25)
    spot = 64.0 * (rank - 4.0 * lap) + first + lap
    place4 = 4.0 * (first + lap) + (rank - 4.0 * lap)

    def pick(values):
        out = jnp.zeros((CAND, 128), F32)
        for r in range(PASS_DEV):
            part = slice(r * CAND, (r + 1) * CAND)
            out = out + hit[part] * values[part]
        return out

    slot = jnp.where(own > 0, pick(spot), -1.0)
    place4 = pick(place4)
    cand = iota((CAND, 128), 0).astype(F32)
    code = CAND * cand + jnp.where(own > 0, local, 0.0)

    own_bf = own.astype(BF16)
    c_i, c_j = iota((CAND, CAND), 0), iota((CAND, CAND), 1)
    count = dot(jnp.ones((CAND, CAND), BF16), own_bf)
    earlier = dot(count.astype(BF16), before)
    entry = earlier + dot(ind(c_j < c_i, BF16), own_bf)
    entry = jnp.where(own > 0, entry, -1.0)
    last_entry = jnp.where(count > 0, earlier + count - 1.0, -1.0)

    lane = iota((8, 128), 1)
    query = ((lane // 8) * Q_DEV + lax.rem(lane, 8)).astype(F32).astype(BF16)
    one8 = jnp.ones((8, 128), BF16)
    qn, codes, valid, entry_place, entry_q = [], [], [], [], []
    for j in range(4):
        at = (iota((64, 128), 0) + 64 * j).astype(F32)
        acc = [jnp.zeros((64, 128), F32) for _ in range(4)]
        for c in range(CAND):
            one = ind(at == slot[c : c + 1])
            acc[0] = acc[0] + one
            acc[1] = acc[1] + one * code[c : c + 1]
            one = ind(at == entry[c : c + 1])
            acc[2] = acc[2] + one * place4[c : c + 1]
            acc[3] = acc[3] + one
        acc = [a.astype(BF16) for a in acc]
        hit_ref[64 * j : 64 * j + 64] = acc[0]
        qn.append(acc[0])
        codes.append(acc[1])
        entry_place.append(acc[2])
        entry_q.append(acc[3])
    at_slot = jnp.concatenate(qn, axis=0)
    qn = dot_nt(query, at_slot)
    valid = dot_nt(one8, at_slot)
    codes = dot_nt(one8, jnp.concatenate(codes, axis=0))
    entry_place = dot_nt(one8, jnp.concatenate(entry_place, axis=0))
    entry_q = dot_nt(query, jnp.concatenate(entry_q, axis=0))
    cands = jnp.floor(codes / CAND)
    row_of = codes - CAND * cands
    cands = jnp.where(valid > 0, cands, -1.0)

    last_group = jnp.where(number > 0, first + groups, 0.0)
    big = iota((256, 128), 0)
    diag = (big == iota((256, 128), 1) * CAND) & (iota((256, 128), 1) < PASS_DEV)
    last_row = dot(jnp.ones((8, 256), BF16), jnp.where(diag, last_group, 0.0).astype(BF16)) - 1.0
    pad = jnp.zeros((8, 128), F32)
    last_row = jnp.concatenate([last_row, pad], axis=1)
    last_entry = jnp.concatenate([last_entry[:8], pad], axis=1)

    sub = iota((8, SLOTS), 0)
    table = jnp.zeros((8, SLOTS), F32)
    rows_of_table = (qn, row_of, entry_place, entry_q, last_row, last_entry, cands)
    most = (OWNERS * Q_DEV - 1, PASS_DEV - 1, 4 * GROUPS - 1, OWNERS * Q_DEV - 1, GROUPS - 1, ENTRIES - 1, CAND - 1)
    for n, values in enumerate(rows_of_table):
        table = jnp.where(sub == n, jnp.clip(values, -1.0, most[n]), table)
    tab_ref[...] = jnp.clip(table.astype(I32), -1, SLOTS - 1)


FAR = (4, 3, 5, 2, 6, 1, 7)
A_ROWS, B_ROWS = 64, 32
A_PIECE, B_PIECE = NY * A_ROWS, NX * B_ROWS
B_AT = NX * A_PIECE
FLAT = PASS_DEV * ROWS


def rows_at(start, count):
    return pl.ds(pl.multiple_of(start, 16), count)


class Swap:
    def __init__(self, n, at, device, send, recv):
        self.n, self.at, self.device, self.send, self.recv = n, at, device, send, recv

    def start(self, src_of, buf):
        self.buf, self.copies = buf, []
        far = sorted(range(1, self.n), key=lambda k: -min(k, self.n - k))
        for k in far:
            t = lax.rem(self.at + k, self.n)
            copy = remote(
                src_of(t), buf.at[self.at], self.send.at[k - 1], self.recv.at[self.at], self.device(t)
            )
            copy.start()
            self.copies.append(copy)

    def finish(self):
        for k in range(1, self.n):
            t = lax.rem(self.at + k, self.n)
            remote(
                self.buf.at[t], self.buf.at[t], self.send.at[0], self.recv.at[t], self.device(t)
            ).wait_recv()

    def drain(self):
        for copy in self.copies:
            copy.wait_send()


def gather_kernel(
    hidden_ref, weight_ref, cache_ref, ids_ref, map_ref,
    query_ref, full_ref, raw_ref, tab_ref, hit_ref, tiles,
    rows_buf, cache_f, w_send, w_recv, r_send, r_recv, q_send, q_recv,
):
    place = Place()
    me = place.me
    barrier = pltpu.get_barrier_semaphore()
    peers = [{"passage": place.ring(k)} for k in NEAR] + [{"passage": place.sibling}]
    for device in peers:
        pl.semaphore_signal(barrier, inc=1, device_id=device, device_id_type=pl.DeviceIdType.MESH)

    full_ref[me] = weight_ref[...]
    table = jnp.broadcast_to(map_ref[...].astype(F32), (8, 256)).astype(BF16)
    own = jnp.full((8, CAND), -1.0, F32)
    for q in range(Q_DEV):
        one = ind(iota((256, CAND), 0) == ids_ref[q : q + 1, :], BF16)
        own = jnp.where(iota((8, CAND), 0) == q, dot(table, one), own)
    rows_buf[me] = jnp.full((8, 128), -1.0, F32)
    rows_buf[me, :, 0:CAND] = own
    pl.semaphore_wait(barrier, len(peers))

    weights = Gather(place, full_ref, w_send, w_recv)
    weights.start()
    rows = Gather(place, rows_buf, r_send, r_recv)
    rows.start()

    cache_f[...] = cache_ref[...].reshape(PLEN * PASS_DEV, DIM).astype(F32)
    for r in range(PASS_DEV):
        tiles[r, ROWS - 16 : ROWS] = jnp.zeros((16, DIM), BF16)
        tiles[r, 0:PLEN] = cache_f[pl.ds(r, PLEN, stride=PASS_DEV), :].astype(BF16)

    weights.finish()
    raw = dot(hidden_ref[...], full_ref[...].reshape(-1, DIM))
    raw_ref[...] = raw
    inverse = lax.rsqrt(jnp.mean(raw * raw, axis=-1, keepdims=True) + EPS)
    query_ref[me] = (raw * inverse).astype(BF16)
    queries = Gather(place, query_ref, q_send, q_recv)
    queries.start()

    rows.finish()
    routing_tables(rows_buf[...].reshape(OWNERS * 8, 128), me, tab_ref, hit_ref)
    queries.finish()


def pair_kernel(
    hidden_ref, full_ref, raw_ref, tiles, len_ref, tab, tab_vec, hit_ref, query_ref,
    hid_ref, wg_ref, cache_out,
    cache_f, exps, logs, recips, scales,
    score_buf, grad_vec, grad_tab, cg_run, qg_group, qg_run, qg_ref, cg_ref,
    ax_buf, ay_buf, by_buf, bx_buf, mid_a, mid_b, fin, q_sib, q_out, q_in, w_own, w_sib, w_out, w_in, w_x, w_y,
    grad_sem, out_sem,
    s_send, s_recv,
    qs_send, qs_recv, qz_send, qz_recv, ws_send, ws_recv, wz_send, wz_recv, wx_send, wx_recv, wy_send, wy_recv,
    a1_send, a1_recv, a2_send, a2_recv, a3_send, a3_recv, a4_send, a4_recv,
    b1_send, b1_recv, b2_send, b2_recv, b3_send, b3_recv, b4_send, b4_recv,
):
    place = Place()
    me, z, c = place.me, place.z, place.c
    dp = lax.axis_index("dp")
    ix, iy = dp // NY, lax.rem(dp, NY)
    others = [lax.rem(me + k, OWNERS) for k in range(1, OWNERS)]
    to_x = lambda k: {"dp": lax.rem(ix + k, NX) * NY + iy}
    to_y = lambda k: {"dp": ix * NY + lax.rem(iy + k, NY)}
    sibling = {"passage": place.sibling}
    similarity_scale = 1.0 / (TAU * math.sqrt(DIM))
    root_scale = 1.0 / math.sqrt(DIM)

    barrier = pltpu.get_barrier_semaphore()
    peers = [{"passage": d} for d in others]
    peers += [to_x(k) for k in range(1, NX)] + [to_y(k) for k in range(1, NY)]
    for device in peers:
        pl.semaphore_signal(barrier, inc=1, device_id=device, device_id_type=pl.DeviceIdType.MESH)
    logs[...] = jnp.zeros_like(logs)
    recips[...] = jnp.zeros_like(recips)

    def bounded(value, most):
        return jnp.minimum(jnp.maximum(value, 0), most)

    def row_of(g):
        return bounded(tab[1, g], PASS_DEV - 1)

    def load_queries(g):
        parts = []
        for j in range(4):
            n = bounded(tab[0, 64 * j + g], OWNERS * Q_DEV - 1)
            parts.append(query_ref[n])
        return jnp.concatenate(parts, axis=0)

    live = iota((ROWS, 128), 0)

    def forward(i, _):
        for u in range(4):
            g = 4 * i + u
            row = row_of(g)
            sims = dot_nt(tiles[row], load_queries(g)) * similarity_scale
            sims = jnp.where(live < len_ref[row], sims, NEG)
            top = jnp.max(sims, axis=0, keepdims=True)
            e = jnp.exp(sims - top)
            total = jnp.sum(e, axis=0, keepdims=True)
            exps[g] = e
            logs[pl.ds(g, 1), :] = top + jnp.log(total)
            recips[pl.ds(g, 1), :] = 1.0 / total
        return 0

    lax.fori_loop(0, GROUPS // 4, forward, 0)

    of_place = iota((SLOTS, 128), 1) // QL == iota((SLOTS, 128), 0) // 64
    spread = jnp.where(of_place, jnp.concatenate([logs[...]] * 4, axis=0), 0.0)
    one8 = jnp.ones((8, 128), BF16)
    score_row = TAU * sum(dot_nt(one8, part) for part in pieces(spread))
    cands = tab_vec[6:7, :]
    is_cand = ind(iota((CAND, SLOTS), 0) == cands)
    hits = hit_ref[...]
    mine = sum(
        dot((is_cand * part[0:1].astype(F32)).astype(BF16), hits) for part in pieces(score_row)
    )
    score_buf[me] = mine[0:8] + pltpu.roll(mine[8:16], 4, 1)
    pl.semaphore_wait(barrier, len(peers))
    score_swap = Swap(OWNERS, me, lambda t: {"passage": t}, s_send, s_recv)
    score_swap.start(lambda t: score_buf.at[me], score_buf)

    def products(i, _):
        for u in range(4):
            g = 4 * i + u
            w = (exps[g] * recips[pl.ds(g, 1), :]).astype(BF16)
            qg_group[g] = dot_tn(w, tiles[row_of(g)]).reshape(4, QL, DIM)
        return 0

    lax.fori_loop(0, GROUPS // 4, products, 0)

    score_swap.finish()
    scores = score_buf[0]
    for d in range(1, OWNERS):
        scores = scores + score_buf[d]
    lane = iota((8, 128), 1)
    low = lax.rem(lane, 8) < Q_DEV

    def both(x, op):
        return op(x, jnp.where(low, pltpu.roll(x, 124, 1), pltpu.roll(x, 4, 1)))

    top = both(jnp.broadcast_to(jnp.max(scores, axis=0, keepdims=True), (8, 128)), jnp.maximum)
    e = jnp.exp(scores - top)
    total = both(jnp.broadcast_to(jnp.sum(e, axis=0, keepdims=True), (8, 128)), jnp.add)
    grad = e / total - ind((iota((8, 128), 0) == 0) & low)
    grad = jnp.concatenate(
        [jnp.where(low, grad, 0.0), jnp.where(low, pltpu.roll(grad, 124, 1), 0.0)], axis=0
    )
    at_slot = is_cand * sum(dot_nt(part, hits) for part in pieces(grad))
    at_slot = jnp.sum(at_slot, axis=0, keepdims=True)
    grad_vec[...] = jnp.broadcast_to(at_slot * root_scale, (8, SLOTS))
    grad_copy = pltpu.make_async_copy(grad_vec, grad_tab, grad_sem)
    grad_copy.start()
    same_group = ind(lax.rem(iota((64, SLOTS), 1), 64) == iota((64, SLOTS), 0))
    to_lanes = ind(of_place, BF16)
    by_lane = sum(dot(part, to_lanes) for part in pieces(same_group * at_slot))
    scales[...] = by_lane * recips[...] * root_scale
    grad_copy.wait()

    def entry_step(i, run):
        for u in range(4):
            e = 4 * i + u
            at = bounded(tab[2, e], 4 * GROUPS - 1)
            group, spot = at // 4, lax.rem(at, 4)
            again = (tab[3, e] == tab[3, jnp.maximum(e - 1, 0)]) & (e > 0)
            run = jnp.where(again, run, 0.0) + qg_group[group, spot] * grad_tab[0, 64 * spot + group]
            qg_run[e] = run
        return run

    lax.fori_loop(0, ENTRIES // 4, entry_step, jnp.zeros((QL, DIM), F32))

    def finish_query(d, _):
        for q in range(Q_DEV):
            last = tab[5, 8 * d + q]
            value = jnp.where(last >= 0, qg_run[bounded(last, ENTRIES - 1)], 0.0)
            qg_ref[d // NC, lax.rem(d, NC), q * QL : (q + 1) * QL, :] = value.astype(BF16)
        return 0

    lax.fori_loop(0, OWNERS, finish_query, 0)
    q_pair = remote(qg_ref.at[:, 1 - c], q_sib, qs_send, qs_recv, sibling)
    q_pair.start()

    def cache_step(i, run):
        for u in range(4):
            g = 4 * i + u
            row = tab[1, g]
            w = (exps[g] * scales[pl.ds(g, 1), :]).astype(BF16)
            again = (row == tab[1, jnp.maximum(g - 1, 0)]) & (g > 0)
            cg_run[g + 1] = jnp.where(again, cg_run[g], 0.0) + dot(w, load_queries(g))
        return run

    lax.fori_loop(0, 4, cache_step, 0)
    q_pair.wait_recv()
    for t in range(NZ):
        q_out[t] = (qg_ref[t, c].astype(F32) + q_sib[t].astype(F32)).astype(BF16)
    on_z = lambda t: {"passage": t * NC + c}
    q_swap = Swap(NZ, z, on_z, qz_send, qz_recv)
    q_swap.start(lambda t: q_out.at[t], q_in)
    lax.fori_loop(4, GROUPS // 4, cache_step, 0)

    for r in range(PASS_DEV):
        last = tab[4, r]
        value = jnp.where(last >= 0, cg_run[bounded(last, GROUPS - 1) + 1], 0.0)
        cache_f[pl.ds(r, ROWS, stride=PASS_DEV), :] = value
    cg_ref[...] = cache_f[...].astype(BF16)

    sent = []

    def push(src, dst, send, recv, device):
        copy = remote(src, dst, send, recv, device)
        copy.start()
        sent.append(copy)

    def await_recv(dst, send, recv):
        remote(dst, dst, send, recv, sibling).wait_recv()

    def y_at(k):
        return lax.rem(iy + k + NY, NY)

    def x_at(k):
        return lax.rem(ix + k + NX, NX)

    for k in FAR:
        src = cg_ref.at[rows_at(B_AT + y_at(k) * B_PIECE, B_PIECE), :]
        push(src, by_buf.at[k - 1], b1_send.at[k - 1], b1_recv.at[k - 1], to_y(k))
    for d in FAR + (0,):
        for k in (2, 1, 3):
            src = cg_ref.at[rows_at(x_at(k) * A_PIECE + y_at(d) * A_ROWS, A_ROWS), :]
            push(src, ax_buf.at[k - 1, d], a1_send.at[k - 1, d], a1_recv.at[k - 1, d], to_x(k))

    q_swap.finish()
    query_gradient = q_out[z].astype(F32)
    for k in range(1, NZ):
        query_gradient = query_gradient + q_in[lax.rem(z + k, NZ)].astype(F32)
    raw = raw_ref[...]
    inverse = lax.rsqrt(jnp.mean(raw * raw, axis=-1, keepdims=True) + EPS)
    mean_term = jnp.mean(query_gradient * raw, axis=-1, keepdims=True)
    raw_grad = (
        inverse * query_gradient - raw * (inverse * inverse * inverse) * mean_term
    ).astype(BF16)
    weight_part = dot_tn(hidden_ref[...], raw_grad)
    w_own[...] = weight_part.astype(BF16).reshape(w_own.shape)
    w_pair = remote(w_own.at[:, 1 - c], w_sib, ws_send, ws_recv, sibling)
    w_pair.start()

    def a_first(d):
        total = cg_ref[rows_at(ix * A_PIECE + y_at(d) * A_ROWS, A_ROWS), :].astype(F32)
        for k in range(1, NX):
            await_recv(ax_buf.at[k - 1, d], a1_send.at[k - 1, d], a1_recv.at[k - 1, d])
            total = total + ax_buf[k - 1, d].astype(F32)
        mid_a[d] = total.astype(BF16)
        if d:
            push(mid_a.at[d], ay_buf.at[d - 1], a2_send.at[d - 1], a2_recv.at[d - 1], to_y(d))

    for d in FAR[:4]:
        a_first(d)
    w_pair.wait_recv()
    for t in range(NZ):
        w_out[t] = (w_own[t, c].astype(F32) + w_sib[t].astype(F32)).astype(BF16)
    w_swap = Swap(NZ, z, on_z, wz_send, wz_recv)
    w_swap.start(lambda t: w_out.at[t], w_in)
    for d in FAR[4:] + (0,):
        a_first(d)
    hid_ref[...] = dot_nt(raw_grad, full_ref[...].reshape(-1, DIM)).astype(BF16)

    total = cg_ref[rows_at(B_AT + iy * B_PIECE, B_PIECE), :].astype(F32)
    for k in range(1, NY):
        await_recv(by_buf.at[k - 1], b1_send.at[k - 1], b1_recv.at[k - 1])
        total = total + by_buf[k - 1].astype(F32)
    mid_b[...] = total.astype(BF16)
    for k in (2, 1, 3):
        src = mid_b.at[rows_at(x_at(k) * B_ROWS, B_ROWS), :]
        push(src, bx_buf.at[k - 1], b2_send.at[k - 1], b2_recv.at[k - 1], to_x(k))
    total = mid_b[rows_at(ix * B_ROWS, B_ROWS), :].astype(F32)
    for k in range(1, NX):
        await_recv(bx_buf.at[k - 1], b2_send.at[k - 1], b2_recv.at[k - 1])
        total = total + bx_buf[k - 1].astype(F32)
    b_span = lambda kx, ky: fin.at[rows_at(B_AT + y_at(ky) * B_PIECE + x_at(kx) * B_ROWS, B_ROWS), :]
    fin[rows_at(B_AT + iy * B_PIECE + ix * B_ROWS, B_ROWS), :] = total.astype(BF16)
    for k in (2, 1, 3):
        push(b_span(0, 0), b_span(0, 0), b3_send.at[k - 1], b3_recv.at[k - 1], to_x(k))

    total = mid_a[0].astype(F32)
    for d in range(1, NY):
        await_recv(ay_buf.at[d - 1], a2_send.at[d - 1], a2_recv.at[d - 1])
        total = total + ay_buf[d - 1].astype(F32)
    a_span = lambda kx, ky: fin.at[rows_at(x_at(kx) * A_PIECE + y_at(ky) * A_ROWS, A_ROWS), :]
    fin[rows_at(ix * A_PIECE + iy * A_ROWS, A_ROWS), :] = total.astype(BF16)
    for d in FAR:
        push(a_span(0, 0), a_span(0, 0), a3_send.at[d - 1], a3_recv.at[d - 1], to_y(d))
    for k in (2, 1, 3):
        push(a_span(0, 0), a_span(0, 0), a4_send.at[k - 1, 0], a4_recv.at[k - 1, 0], to_x(k))

    w_swap.finish()
    total = w_out[z].astype(F32)
    for k in range(1, NZ):
        total = total + w_in[lax.rem(z + k, NZ)].astype(F32)
    w_x[ix] = total.astype(BF16)
    x_swap = Swap(NX, ix, lambda t: {"dp": t * NY + iy}, wx_send, wx_recv)
    x_swap.start(lambda t: w_x.at[ix], w_x)

    for k in range(1, NX):
        await_recv(b_span(-k, 0), b3_send.at[k - 1], b3_recv.at[k - 1])
    b_line = lambda k: fin.at[rows_at(B_AT + y_at(k) * B_PIECE, B_PIECE), :]
    for d in FAR:
        push(b_line(0), b_line(0), b4_send.at[d - 1], b4_recv.at[d - 1], to_y(d))

    def a_forward(d):
        await_recv(a_span(0, -d), a3_send.at[d - 1], a3_recv.at[d - 1])
        for k in (2, 1, 3):
            push(a_span(0, -d), a_span(0, -d), a4_send.at[k - 1, d], a4_recv.at[k - 1, d], to_x(k))

    for d in NEAR[:4]:
        a_forward(d)
    x_swap.finish()
    total = w_x[0].astype(F32)
    for t in range(1, NX):
        total = total + w_x[t].astype(F32)
    w_y[iy] = total.astype(BF16)
    y_swap = Swap(NY, iy, lambda t: {"dp": ix * NY + t}, wy_send, wy_recv)
    y_swap.start(lambda t: w_y.at[iy], w_y)
    for d in NEAR[4:]:
        a_forward(d)

    for d in range(1, NY):
        await_recv(b_line(-d), b4_send.at[d - 1], b4_recv.at[d - 1])
    b_live = PLEN * PASS_DEV - B_AT
    b_out = pltpu.make_async_copy(
        fin.at[pl.ds(B_AT, b_live), :], cache_out.at[pl.ds(B_AT, b_live), :], out_sem.at[0]
    )
    b_out.start()
    for d in range(NY):
        for k in range(1, NX):
            await_recv(a_span(-k, -d), a4_send.at[k - 1, d], a4_recv.at[k - 1, d])
    a_out = pltpu.make_async_copy(
        fin.at[pl.ds(0, B_AT), :], cache_out.at[pl.ds(0, B_AT), :], out_sem.at[1]
    )
    a_out.start()
    y_swap.finish()
    total = w_y[0].astype(F32)
    for t in range(1, NY):
        total = total + w_y[t].astype(F32)
    wg_ref[...] = total

    q_pair.wait_send()
    w_pair.wait_send()
    for moved in (score_swap, q_swap, w_swap, x_swap, y_swap):
        moved.drain()
    for copy in sent:
        copy.wait_send()
    b_out.wait()
    a_out.wait()


VMEM = pl.BlockSpec(memory_space=pltpu.VMEM)
SMEM = pl.BlockSpec(memory_space=pltpu.SMEM)
ANY = pl.BlockSpec(memory_space=pl.ANY)


def call(kernel, collective_id, out_shape, in_specs, out_specs, scratch, args):
    return pl.pallas_call(
        kernel,
        out_shape=out_shape,
        in_specs=in_specs,
        out_specs=out_specs,
        scratch_shapes=scratch,
        compiler_params=pltpu.CompilerParams(
            collective_id=collective_id, has_side_effects=True, vmem_limit_bytes=56 * 2**20
        ),
    )(*args)


def shards(hidden, weight, cache, lengths, passage_ids, owner_map):
    width = hidden.shape[-1]
    share = width // OWNERS
    tokens = Q_DEV * QL
    shape = jax.ShapeDtypeStruct
    dma = pltpu.SemaphoreType.DMA
    vmem = pltpu.VMEM

    def pair(*sizes):
        return [dma(sizes), dma(sizes)]

    gather = [dma((2 * NZ - 1,)), dma((OWNERS,))]
    hidden = hidden.reshape(tokens, width)
    queries, full, raw, tab, hits, tiles = call(
        gather_kernel,
        0,
        [
            shape((OWNERS, tokens, DIM), BF16),
            shape((OWNERS, share, DIM), BF16),
            shape((tokens, DIM), F32),
            shape((8, SLOTS), I32),
            shape((SLOTS, 128), BF16),
            shape((PASS_DEV, ROWS, DIM), BF16),
        ],
        [VMEM] * 5,
        [VMEM] * 6,
        [vmem((OWNERS, 8, 128), F32), vmem((PLEN * PASS_DEV, DIM), F32)] + gather + gather + gather,
        (hidden, weight, jnp.transpose(cache, (1, 0, 2)), passage_ids, owner_map.reshape(1, -1)),
    )
    scratch = [
        vmem((FLAT, DIM), F32),
        vmem((GROUPS, ROWS, 128), F32),
        vmem((64, 128), F32),
        vmem((64, 128), F32),
        vmem((64, 128), F32),
        vmem((OWNERS, 8, 128), F32),
        vmem((8, SLOTS), F32),
        pltpu.SMEM((8, SLOTS), F32),
        vmem((GROUPS + 1, ROWS, DIM), F32),
        vmem((GROUPS, 4, QL, DIM), F32),
        vmem((ENTRIES, QL, DIM), F32),
        vmem((NZ, NC, tokens, DIM), BF16),
        vmem((FLAT, DIM), BF16),
        vmem((NX - 1, NY, A_ROWS, DIM), BF16),
        vmem((NY - 1, A_ROWS, DIM), BF16),
        vmem((NY - 1, B_PIECE, DIM), BF16),
        vmem((NX - 1, B_ROWS, DIM), BF16),
        vmem((NY, A_ROWS, DIM), BF16),
        vmem((B_PIECE, DIM), BF16),
        vmem((FLAT, DIM), BF16),
        vmem((NZ, tokens, DIM), BF16),
        vmem((NZ, tokens, DIM), BF16),
        vmem((NZ, tokens, DIM), BF16),
        vmem((NZ, NC, share, DIM), BF16),
        vmem((NZ, share, DIM), BF16),
        vmem((NZ, share, DIM), BF16),
        vmem((NZ, share, DIM), BF16),
        vmem((NX, share, DIM), BF16),
        vmem((NY, share, DIM), BF16),
        dma,
        dma((2,)),
    ]
    swap = lambda n: [dma((n - 1,)), dma((n,))]
    scratch += swap(OWNERS)
    scratch += [dma, dma] + swap(NZ) + [dma, dma] + swap(NZ) + swap(NX) + swap(NY)
    scratch += pair(NX - 1, NY) + pair(NY - 1) + pair(NY - 1) + pair(NX - 1, NY)
    scratch += pair(NY - 1) + pair(NX - 1) + pair(NX - 1) + pair(NY - 1)

    hid, wg, cache_grad = call(
        pair_kernel,
        1,
        [
            shape((tokens, width), BF16),
            shape((share, DIM), F32),
            shape((PLEN * PASS_DEV, DIM), BF16),
        ],
        [VMEM, VMEM, VMEM, VMEM, SMEM, SMEM, VMEM, VMEM, VMEM],
        [VMEM, VMEM, ANY],
        scratch,
        (hidden, full, raw, tiles, lengths, tab, tab, hits, queries.reshape(OWNERS * Q_DEV, QL, DIM)),
    )
    cache_grad = jnp.transpose(cache_grad.reshape(PLEN, PASS_DEV, DIM), (1, 0, 2))
    return hid.reshape(Q_DEV, QL, width), wg, cache_grad


def solution(mesh):
    in_specs = (
        P(("dp", "passage"), None, None),
        P("passage", None),
        P("passage", None, None),
        P("passage"),
        P(("dp", "passage"), None),
        P(),
    )
    out_specs = (P(("dp", "passage"), None, None), P("passage", None), P("passage", None, None))
    return jax.shard_map(shards, mesh=mesh, in_specs=in_specs, out_specs=out_specs, check_vma=False)
```

time: 118 us -> 89 us (0.75)
  the two profiles are of different devices: /device:TPU:8 before, /device:TPU:1 now
where the time goes in v2:
time: 89 us; the launch traced here: 87.3 us
  Pallas kernels  82.3 us (92%)
  local copies, waits for them, and re-layouts  4.34 us (5%)
    pallas_call x2, Pallas kernels, call(): pl.pallas_call(kernel, out_shape=out_shape, in_specs=in_specs, out_specs=...  82.3 us
    unnamed x5, local copies, waits for them, and re-layouts  4.34 us

profile of v2, /device:TPU:1, one launch (start us, length us, event | category | flops | bytes accessed | tf_op | source)
XLA Modules:
  0.0 87.3 jit_solution(2382523558147337499)
XLA Ops:
  0.6 31.6 %shard_map.85 = (bf16[16,128,128]{2,1,0:T(8,128)(2,1)}, bf16[16,48,128]{2,1,0:T(8,128)(2,1)}, f32[128,128]{1,0:T(8,128)}, s32[8,256]{1,0:T(8,128)}, bf16[256,128...) custom-call(bf16[128,768]{1,0:T(8,128)(2,1)} %bitcast.8, bf16[48,128]{1,0:T(8,128)(2,1)} %weight_ref.1, ...), custom_call_target="tpu_custom_call" | custom-call | tf_op jit(solution)/shard_map/pallas_call | solution.py:604
  32.2 50.7 %shard_map.86 = (bf16[128,768]{1,0:T(8,128)(2,1)}, f32[48,128]{1,0:T(8,128)}, bf16[2880,128]{1,0:T(8,128)(2,1)}) custom-call(bf16[128,768]{1,0:T(8,128)(2,1)} %bitcast.9, bf16[16,48,128]{2,1,0:T(8,128)(2,1)} %get-tuple-element.12.full_ref, f32[128,128]{1,0:T(8,128)} %get-tuple-element.13.raw_ref, bf16[16,192,128]{2,1,0:T(8,128)(2,1)} %get-tuple-element.14.tiles, ...), custom_call_target="tpu_custom_call" | custom-call | tf_op jit(solution)/shard_map/pallas_call | solution.py:604
  82.9 0.0 copy-start
  82.9 1.6 %copy.12 = bf16[4,32,768]{2,1,0:T(8,128)(2,1)} copy(bf16[4,32,768]{2,1,0:T(8,128)(2,1)} %bitcast.13) | data formatting | bytes 393216
  84.6 0.0 copy-done
  84.6 0.6 copy.13
  85.2 2.1 %copy.14 = bf16[16,180,128]{2,0,1:T(8,128)(2,1)} copy(bf16[16,180,128]{2,0,1:T(8,128)(2,1)} %bitcast.11) | data formatting | bytes 1474560
Async XLA Ops:
  82.9 1.6 %copy-start = (f32[48,128]{1,0:T(8,128)S(1)}, f32[48,128]{1,0:T(8,128)}, u32[]{:S(2)}) copy-start(f32[48,128]{1,0:T(8,128)} %get-tuple-element.25) | copy-start | bytes 73732

commit v3 on v2

--- a/solution.py
+++ b/solution.py
@@ -97,16 +97,19 @@
         self.sent.append(self.copy(p.me, NZ - 1, p.sibling))
         self.sent[-1].start()
 
-    def finish(self):
+    def finish(self, landed=lambda slot: None):
         p = self.place
         for n, k in enumerate(NEAR):
             forward = self.copy(p.ring(k), NZ + n, p.sibling)
             forward.wait_recv()
             forward.start()
             self.sent.append(forward)
+            landed(p.ring(k))
         self.copy(p.sibling, 0, p.sibling).wait_recv()
+        landed(p.sibling)
         for k in NEAR:
             self.copy(p.ring_sibling(k), 0, p.sibling).wait_recv()
+            landed(p.ring_sibling(k))
         for copy in self.sent:
             copy.wait_send()
 
@@ -242,9 +245,10 @@
 
 
 def gather_kernel(
-    hidden_ref, weight_ref, cache_ref, ids_ref, map_ref,
-    query_ref, full_ref, raw_ref, tab_ref, hit_ref, tiles,
-    rows_buf, cache_f, w_send, w_recv, r_send, r_recv, q_send, q_recv,
+    hidden_hbm, weight_ref, cache_hbm, ids_ref, map_ref,
+    query_out, full_out, raw_ref, tab_ref, hit_ref, tiles_out,
+    hidden_ref, cache_ref, query_ref, full_ref, tiles,
+    rows_buf, cache_f, in_sem, tiles_sem, full_sem, query_sem, w_send, w_recv, r_send, r_recv, q_send, q_recv,
 ):
     place = Place()
     me = place.me
@@ -253,6 +257,10 @@
     for device in peers:
         pl.semaphore_signal(barrier, inc=1, device_id=device, device_id_type=pl.DeviceIdType.MESH)
 
+    hidden_in = pltpu.make_async_copy(hidden_hbm, hidden_ref, in_sem.at[0])
+    cache_in = pltpu.make_async_copy(cache_hbm, cache_ref, in_sem.at[1])
+    hidden_in.start()
+    cache_in.start()
     full_ref[me] = weight_ref[...]
     table = jnp.broadcast_to(map_ref[...].astype(F32), (8, 256)).astype(BF16)
     own = jnp.full((8, CAND), -1.0, F32)
@@ -268,12 +276,18 @@
     rows = Gather(place, rows_buf, r_send, r_recv)
     rows.start()
 
+    cache_in.wait()
     cache_f[...] = cache_ref[...].reshape(PLEN * PASS_DEV, DIM).astype(F32)
     for r in range(PASS_DEV):
         tiles[r, ROWS - 16 : ROWS] = jnp.zeros((16, DIM), BF16)
         tiles[r, 0:PLEN] = cache_f[pl.ds(r, PLEN, stride=PASS_DEV), :].astype(BF16)
 
+    tiles_copy = pltpu.make_async_copy(tiles, tiles_out, tiles_sem)
+    tiles_copy.start()
+    hidden_in.wait()
     weights.finish()
+    full_copy = pltpu.make_async_copy(full_ref, full_out, full_sem)
+    full_copy.start()
     raw = dot(hidden_ref[...], full_ref[...].reshape(-1, DIM))
     raw_ref[...] = raw
     inverse = lax.rsqrt(jnp.mean(raw * raw, axis=-1, keepdims=True) + EPS)
@@ -283,12 +297,23 @@
 
     rows.finish()
     routing_tables(rows_buf[...].reshape(OWNERS * 8, 128), me, tab_ref, hit_ref)
-    queries.finish()
+    kept = []
+
+    def keep(slot):
+        copy = pltpu.make_async_copy(query_ref.at[slot], query_out.at[slot], query_sem.at[slot])
+        copy.start()
+        kept.append(copy)
+
+    keep(me)
+    queries.finish(keep)
+    for copy in kept + [tiles_copy, full_copy]:
+        copy.wait()
 
 
 def pair_kernel(
-    hidden_ref, full_ref, raw_ref, tiles, len_ref, tab, tab_vec, hit_ref, query_ref,
+    hidden_hbm, full_hbm, raw_hbm, tiles_hbm, len_ref, tab, tab_hbm, hit_hbm, query_hbm,
     hid_ref, wg_ref, cache_out,
+    hidden_ref, full_ref, raw_ref, tiles, tab_vec, hit_ref, query_ref, in_sem,
     cache_f, exps, logs, recips, scales,
     score_buf, grad_vec, grad_tab, cg_run, qg_group, qg_run, qg_ref, cg_ref,
     ax_buf, ay_buf, by_buf, bx_buf, mid_a, mid_b, fin, q_sib, q_out, q_in, w_own, w_sib, w_out, w_in, w_x, w_y,
@@ -314,8 +339,26 @@
     peers += [to_x(k) for k in range(1, NX)] + [to_y(k) for k in range(1, NY)]
     for device in peers:
         pl.semaphore_signal(barrier, inc=1, device_id=device, device_id_type=pl.DeviceIdType.MESH)
+    moves = [
+        pltpu.make_async_copy(src, dst, in_sem.at[n])
+        for n, (src, dst) in enumerate(
+            [
+                (tiles_hbm, tiles),
+                (query_hbm, query_ref),
+                (tab_hbm, tab_vec),
+                (hit_hbm, hit_ref),
+                (hidden_hbm, hidden_ref),
+                (full_hbm, full_ref),
+                (raw_hbm, raw_ref),
+            ]
+        )
+    ]
+    for move in moves:
+        move.start()
     logs[...] = jnp.zeros_like(logs)
     recips[...] = jnp.zeros_like(recips)
+    for move in moves[:2]:
+        move.wait()
 
     def bounded(value, most):
         return jnp.minimum(jnp.maximum(value, 0), most)
@@ -347,6 +390,9 @@
         return 0
 
     lax.fori_loop(0, GROUPS // 4, forward, 0)
+
+    for move in moves[2:]:
+        move.wait()
 
     of_place = iota((SLOTS, 128), 1) // QL == iota((SLOTS, 128), 0) // 64
     spread = jnp.where(of_place, jnp.concatenate([logs[...]] * 4, axis=0), 0.0)
@@ -595,6 +641,25 @@
     a_out.wait()
 
 
+def result_kernel(hid, wg, cache, hid_out, wg_out, cache_out, hid_buf, wg_buf, cache_buf, sems):
+    part = PLEN * PASS_DEV // 4
+    moves = []
+    for n in range(4):
+        span = pl.ds(n * part, part)
+        moves.append((cache.at[span, :], cache_buf.at[span, :], cache_out.at[span, :]))
+    moves += [(hid, hid_buf, hid_out), (wg, wg_buf, wg_out)]
+    reads, writes = [], []
+    for n, (src, mid, _) in enumerate(moves):
+        reads.append(pltpu.make_async_copy(src, mid, sems.at[0, n]))
+        reads[-1].start()
+    for n, (_, mid, dst) in enumerate(moves):
+        reads[n].wait()
+        writes.append(pltpu.make_async_copy(mid, dst, sems.at[1, n]))
+        writes[-1].start()
+    for copy in writes:
+        copy.wait()
+
+
 VMEM = pl.BlockSpec(memory_space=pltpu.VMEM)
 SMEM = pl.BlockSpec(memory_space=pltpu.SMEM)
 ANY = pl.BlockSpec(memory_space=pl.ANY)
@@ -637,12 +702,35 @@
             shape((SLOTS, 128), BF16),
             shape((PASS_DEV, ROWS, DIM), BF16),
         ],
-        [VMEM] * 5,
-        [VMEM] * 6,
-        [vmem((OWNERS, 8, 128), F32), vmem((PLEN * PASS_DEV, DIM), F32)] + gather + gather + gather,
+        [ANY, VMEM, ANY, VMEM, VMEM],
+        [ANY, ANY, VMEM, VMEM, VMEM, ANY],
+        [
+            vmem((tokens, width), BF16),
+            vmem((PLEN, PASS_DEV, DIM), BF16),
+            vmem((OWNERS, tokens, DIM), BF16),
+            vmem((OWNERS, share, DIM), BF16),
+            vmem((PASS_DEV, ROWS, DIM), BF16),
+            vmem((OWNERS, 8, 128), F32),
+            vmem((PLEN * PASS_DEV, DIM), F32),
+            dma((2,)),
+            dma,
+            dma,
+            dma((OWNERS,)),
+        ]
+        + gather
+        + gather
+        + gather,
         (hidden, weight, jnp.transpose(cache, (1, 0, 2)), passage_ids, owner_map.reshape(1, -1)),
     )
     scratch = [
+        vmem((tokens, width), BF16),
+        vmem((OWNERS, share, DIM), BF16),
+        vmem((tokens, DIM), F32),
+        vmem((PASS_DEV, ROWS, DIM), BF16),
+        vmem((8, SLOTS), I32),
+        vmem((SLOTS, 128), BF16),
+        vmem((OWNERS * Q_DEV, QL, DIM), BF16),
+        dma((7,)),
         vmem((FLAT, DIM), F32),
         vmem((GROUPS, ROWS, 128), F32),
         vmem((64, 128), F32),
@@ -689,11 +777,18 @@
             shape((share, DIM), F32),
             shape((PLEN * PASS_DEV, DIM), BF16),
         ],
-        [VMEM, VMEM, VMEM, VMEM, SMEM, SMEM, VMEM, VMEM, VMEM],
+        [ANY, ANY, ANY, ANY, SMEM, SMEM, ANY, ANY, ANY],
         [VMEM, VMEM, ANY],
         scratch,
         (hidden, full, raw, tiles, lengths, tab, tab, hits, queries.reshape(OWNERS * Q_DEV, QL, DIM)),
     )
+    hid, wg, cache_grad = pl.pallas_call(
+        result_kernel,
+        out_shape=[shape(x.shape, x.dtype) for x in (hid, wg, cache_grad)],
+        in_specs=[ANY] * 3,
+        out_specs=[ANY] * 3,
+        scratch_shapes=[vmem(x.shape, x.dtype) for x in (hid, wg, cache_grad)] + [dma((2, 6))],
+    )(hid, wg, cache_grad)
     cache_grad = jnp.transpose(cache_grad.reshape(PLEN, PASS_DEV, DIM), (1, 0, 2))
     return hid.reshape(Q_DEV, QL, width), wg, cache_grad
 

time: 89 us -> 86.9 us (0.976)
  local copies, waits for them, and re-layouts: 4.34 us -> 0 us
  Pallas kernels: 82.3 us -> 85.3 us
    unnamed x5 -> x0, local copies, waits for them, and re-layouts: 4.34 us -> none
    pallas_call x0 -> x1, Pallas kernels: none -> 2.04 us  [shards(): pl.pallas_call(result_kernel, out_shape=[shape(x.shape, x.dtype) for x in...]
    pallas_call x2, Pallas kernels: 82.3 us -> 83.3 us  [call(): pl.pallas_call(kernel, out_shape=out_shape, in_specs=in_specs, out_specs=...]
where the time goes in v3:
time: 86.9 us; the launch traced here: 86 us
  Pallas kernels  85.3 us (98%)
    pallas_call x2, Pallas kernels, call(): pl.pallas_call(kernel, out_shape=out_shape, in_specs=in_specs, out_specs=...  83.3 us
    pallas_call x1, Pallas kernels, shards(): pl.pallas_call(result_kernel, out_shape=[shape(x.shape, x.dtype) for x in...  2.04 us

profile of v3, /device:TPU:1, one launch (start us, length us, event | category | flops | bytes accessed | tf_op | source)
XLA Modules:
  0.0 86.0 jit_solution(9758119792382100247)
XLA Ops:
  0.6 31.3 %shard_map.85 = (bf16[16,128,128]{2,1,0:T(8,128)(2,1)}, bf16[16,48,128]{2,1,0:T(8,128)(2,1)}, f32[128,128]{1,0:T(8,128)}, s32[8,256]{1,0:T(8,128)}, bf16[256,128...) custom-call(bf16[128,768]{1,0:T(8,128)(2,1)} %bitcast.8, bf16[48,128]{1,0:T(8,128)(2,1)} %weight_ref.1, ...), custom_call_target="tpu_custom_call" | custom-call | tf_op jit(solution)/shard_map/pallas_call | solution.py:669
  32.0 52.0 %shard_map.86 = (bf16[128,768]{1,0:T(8,128)(2,1)}, f32[48,128]{1,0:T(8,128)}, bf16[2880,128]{1,0:T(8,128)(2,1)}) custom-call(bf16[128,768]{1,0:T(8,128)(2,1)} %bitcast.9, bf16[16,48,128]{2,1,0:T(8,128)(2,1)} %get-tuple-element.15.full_hbm, f32[128,128]{1,0:T(8,128)} %get-tuple-element.16.raw_hbm, bf16[16,192,128]{2,1,0:T(8,128)(2,1)} %get-tuple-element.17.tiles_hbm, ...), custom_call_target="tpu_custom_call" | custom-call | tf_op jit(solution)/shard_map/pallas_call | solution.py:669
  83.9 2.0 %shard_map.87 = (bf16[128,768]{1,0:T(8,128)(2,1)}, f32[48,128]{1,0:T(8,128)}, bf16[2880,128]{1,0:T(8,128)(2,1)}) custom-call(bf16[128,768]{1,0:T(8,128)(2,1)} %get-tuple-element.21.hid, f32[48,128]{1,0:T(8,128)} %get-tuple-element.22.wg, bf16[2880,128]{1,0:T(8,128)(2,1)} %get-tuple-element.23.cache), custom_call_target="tpu_custom_call" | custom-call | tf_op jit(solution)/shard_map/pallas_call | solution.py:785

commit v4 on v2

--- a/solution.py
+++ b/solution.py
@@ -18,7 +18,8 @@
 DIM = 128
 GROUPS = 60
 SLOTS = 256
-ENTRIES = 192
+CAP = 12
+PAIRS = Q_DEV * CAND
 NEG = -1e30
 
 F32, BF16, I32 = jnp.float32, jnp.bfloat16, jnp.int32
@@ -81,7 +82,7 @@
 class Gather:
     def __init__(self, place, buf, send, recv):
         self.place, self.buf, self.send, self.recv = place, buf, send, recv
-        self.sent = []
+        self.sent, self.relayed = [], 0
 
     def copy(self, slot, n, peer):
         return remote(
@@ -91,116 +92,31 @@
 
     def start(self):
         p = self.place
-        for n, k in enumerate(NEAR):
+        for n, k in list(enumerate(NEAR))[::-1]:
             self.sent.append(self.copy(p.me, n, p.ring(k)))
             self.sent[-1].start()
         self.sent.append(self.copy(p.me, NZ - 1, p.sibling))
         self.sent[-1].start()
 
-    def finish(self):
+    def relay(self, upto):
         p = self.place
-        for n, k in enumerate(NEAR):
-            forward = self.copy(p.ring(k), NZ + n, p.sibling)
+        for n in range(self.relayed, upto):
+            forward = self.copy(p.ring(NEAR[n]), NZ + n, p.sibling)
             forward.wait_recv()
             forward.start()
             self.sent.append(forward)
+        self.relayed = upto
+
+    def finish(self):
+        p = self.place
+        self.relay(NZ - 1)
         self.copy(p.sibling, 0, p.sibling).wait_recv()
         for k in NEAR:
             self.copy(p.ring_sibling(k), 0, p.sibling).wait_recv()
+
+    def drain(self):
         for copy in self.sent:
             copy.wait_send()
-
-
-def routing_tables(rows, me, tab_ref, hit_ref):
-    rows_t = dot_nt(ind(iota((CAND, 128), 0) == iota((CAND, 128), 1), BF16), rows.astype(BF16))
-    local = rows_t - (PASS_DEV * me).astype(F32)
-    own = ind((local >= 0) & (local < PASS_DEV))
-    hit = jnp.concatenate([ind(local == r) for r in range(PASS_DEV)], axis=0)
-    lane_i, lane_j = iota((128, 128), 0), iota((128, 128), 1)
-    upto = ind(lane_i <= lane_j, BF16)
-    before = ind(lane_i < lane_j, BF16)
-    ones = jnp.ones((128, 128), BF16)
-    hit_bf = hit.astype(BF16)
-    seen = dot(hit_bf, upto)
-    total = dot(hit_bf, ones).astype(BF16)
-    big_i, big_j = iota((256, 256), 0), iota((256, 256), 1)
-    row_i, row_j = big_i // CAND, big_j // CAND
-    ahead = dot(ind((row_i == row_j) & (big_j < big_i), BF16), total)
-    number = dot(ind(row_i == row_j, BF16), total)
-    groups = jnp.floor((number + 3.0) * 0.25)
-    first = dot(
-        ind((row_j < row_i) & (big_j == row_j * CAND), BF16), groups.astype(BF16)
-    )
-    rank = seen - 1.0 + ahead
-    lap = jnp.floor(rank * 0.25)
-    spot = 64.0 * (rank - 4.0 * lap) + first + lap
-    place4 = 4.0 * (first + lap) + (rank - 4.0 * lap)
-
-    def pick(values):
-        out = jnp.zeros((CAND, 128), F32)
-        for r in range(PASS_DEV):
-            part = slice(r * CAND, (r + 1) * CAND)
-            out = out + hit[part] * values[part]
-        return out
-
-    slot = jnp.where(own > 0, pick(spot), -1.0)
-    place4 = pick(place4)
-    cand = iota((CAND, 128), 0).astype(F32)
-    code = CAND * cand + jnp.where(own > 0, local, 0.0)
-
-    own_bf = own.astype(BF16)
-    c_i, c_j = iota((CAND, CAND), 0), iota((CAND, CAND), 1)
-    count = dot(jnp.ones((CAND, CAND), BF16), own_bf)
-    earlier = dot(count.astype(BF16), before)
-    entry = earlier + dot(ind(c_j < c_i, BF16), own_bf)
-    entry = jnp.where(own > 0, entry, -1.0)
-    last_entry = jnp.where(count > 0, earlier + count - 1.0, -1.0)
-
-    lane = iota((8, 128), 1)
-    query = ((lane // 8) * Q_DEV + lax.rem(lane, 8)).astype(F32).astype(BF16)
-    one8 = jnp.ones((8, 128), BF16)
-    qn, codes, valid, entry_place, entry_q = [], [], [], [], []
-    for j in range(4):
-        at = (iota((64, 128), 0) + 64 * j).astype(F32)
-        acc = [jnp.zeros((64, 128), F32) for _ in range(4)]
-        for c in range(CAND):
-            one = ind(at == slot[c : c + 1])
-            acc[0] = acc[0] + one
-            acc[1] = acc[1] + one * code[c : c + 1]
-            one = ind(at == entry[c : c + 1])
-            acc[2] = acc[2] + one * place4[c : c + 1]
-            acc[3] = acc[3] + one
-        acc = [a.astype(BF16) for a in acc]
-        hit_ref[64 * j : 64 * j + 64] = acc[0]
-        qn.append(acc[0])
-        codes.append(acc[1])
-        entry_place.append(acc[2])
-        entry_q.append(acc[3])
-    at_slot = jnp.concatenate(qn, axis=0)
-    qn = dot_nt(query, at_slot)
-    valid = dot_nt(one8, at_slot)
-    codes = dot_nt(one8, jnp.concatenate(codes, axis=0))
-    entry_place = dot_nt(one8, jnp.concatenate(entry_place, axis=0))
-    entry_q = dot_nt(query, jnp.concatenate(entry_q, axis=0))
-    cands = jnp.floor(codes / CAND)
-    row_of = codes - CAND * cands
-    cands = jnp.where(valid > 0, cands, -1.0)
-
-    last_group = jnp.where(number > 0, first + groups, 0.0)
-    big = iota((256, 128), 0)
-    diag = (big == iota((256, 128), 1) * CAND) & (iota((256, 128), 1) < PASS_DEV)
-    last_row = dot(jnp.ones((8, 256), BF16), jnp.where(diag, last_group, 0.0).astype(BF16)) - 1.0
-    pad = jnp.zeros((8, 128), F32)
-    last_row = jnp.concatenate([last_row, pad], axis=1)
-    last_entry = jnp.concatenate([last_entry[:8], pad], axis=1)
-
-    sub = iota((8, SLOTS), 0)
-    table = jnp.zeros((8, SLOTS), F32)
-    rows_of_table = (qn, row_of, entry_place, entry_q, last_row, last_entry, cands)
-    most = (OWNERS * Q_DEV - 1, PASS_DEV - 1, 4 * GROUPS - 1, OWNERS * Q_DEV - 1, GROUPS - 1, ENTRIES - 1, CAND - 1)
-    for n, values in enumerate(rows_of_table):
-        table = jnp.where(sub == n, jnp.clip(values, -1.0, most[n]), table)
-    tab_ref[...] = jnp.clip(table.astype(I32), -1, SLOTS - 1)
 
 
 FAR = (4, 3, 5, 2, 6, 1, 7)
@@ -241,59 +157,16 @@
             copy.wait_send()
 
 
-def gather_kernel(
-    hidden_ref, weight_ref, cache_ref, ids_ref, map_ref,
-    query_ref, full_ref, raw_ref, tab_ref, hit_ref, tiles,
-    rows_buf, cache_f, w_send, w_recv, r_send, r_recv, q_send, q_recv,
-):
-    place = Place()
-    me = place.me
-    barrier = pltpu.get_barrier_semaphore()
-    peers = [{"passage": place.ring(k)} for k in NEAR] + [{"passage": place.sibling}]
-    for device in peers:
-        pl.semaphore_signal(barrier, inc=1, device_id=device, device_id_type=pl.DeviceIdType.MESH)
-
-    full_ref[me] = weight_ref[...]
-    table = jnp.broadcast_to(map_ref[...].astype(F32), (8, 256)).astype(BF16)
-    own = jnp.full((8, CAND), -1.0, F32)
-    for q in range(Q_DEV):
-        one = ind(iota((256, CAND), 0) == ids_ref[q : q + 1, :], BF16)
-        own = jnp.where(iota((8, CAND), 0) == q, dot(table, one), own)
-    rows_buf[me] = jnp.full((8, 128), -1.0, F32)
-    rows_buf[me, :, 0:CAND] = own
-    pl.semaphore_wait(barrier, len(peers))
-
-    weights = Gather(place, full_ref, w_send, w_recv)
-    weights.start()
-    rows = Gather(place, rows_buf, r_send, r_recv)
-    rows.start()
-
-    cache_f[...] = cache_ref[...].reshape(PLEN * PASS_DEV, DIM).astype(F32)
-    for r in range(PASS_DEV):
-        tiles[r, ROWS - 16 : ROWS] = jnp.zeros((16, DIM), BF16)
-        tiles[r, 0:PLEN] = cache_f[pl.ds(r, PLEN, stride=PASS_DEV), :].astype(BF16)
-
-    weights.finish()
-    raw = dot(hidden_ref[...], full_ref[...].reshape(-1, DIM))
-    raw_ref[...] = raw
-    inverse = lax.rsqrt(jnp.mean(raw * raw, axis=-1, keepdims=True) + EPS)
-    query_ref[me] = (raw * inverse).astype(BF16)
-    queries = Gather(place, query_ref, q_send, q_recv)
-    queries.start()
-
-    rows.finish()
-    routing_tables(rows_buf[...].reshape(OWNERS * 8, 128), me, tab_ref, hit_ref)
-    queries.finish()
-
-
 def pair_kernel(
-    hidden_ref, full_ref, raw_ref, tiles, len_ref, tab, tab_vec, hit_ref, query_ref,
+    hidden_hbm, weight_ref, cache_hbm, len_ref, ids, owner_of,
     hid_ref, wg_ref, cache_out,
+    hidden_ref, cache_ref, query_ref, full_ref, tiles, rows_buf, rows_vec, rows_tab, count_vec, count_tab,
+    tab_vec, tab, last_tab,
     cache_f, exps, logs, recips, scales,
-    score_buf, grad_vec, grad_tab, cg_run, qg_group, qg_run, qg_ref, cg_ref,
+    score_buf, grad_vec, grad_tab, cg_run, qg_group, qg_ref, cg_ref,
     ax_buf, ay_buf, by_buf, bx_buf, mid_a, mid_b, fin, q_sib, q_out, q_in, w_own, w_sib, w_out, w_in, w_x, w_y,
-    grad_sem, out_sem,
-    s_send, s_recv,
+    in_sem, tab_sem, grad_sem, out_sem,
+    w_send, w_recv, r_send, r_recv, q_send, q_recv, s_send, s_recv,
     qs_send, qs_recv, qz_send, qz_recv, ws_send, ws_recv, wz_send, wz_recv, wx_send, wx_recv, wy_send, wy_recv,
     a1_send, a1_recv, a2_send, a2_recv, a3_send, a3_recv, a4_send, a4_recv,
     b1_send, b1_recv, b2_send, b2_recv, b3_send, b3_recv, b4_send, b4_recv,
@@ -314,20 +187,126 @@
     peers += [to_x(k) for k in range(1, NX)] + [to_y(k) for k in range(1, NY)]
     for device in peers:
         pl.semaphore_signal(barrier, inc=1, device_id=device, device_id_type=pl.DeviceIdType.MESH)
+    hidden_in = pltpu.make_async_copy(hidden_hbm, hidden_ref, in_sem.at[0])
+    cache_in = pltpu.make_async_copy(cache_hbm, cache_ref, in_sem.at[1])
+    hidden_in.start()
+    cache_in.start()
+
+    def bounded(value, most):
+        return jnp.minimum(jnp.maximum(value, 0), most)
+
+    full_ref[me] = weight_ref[...]
+    lane = iota((8, 128), 1)
+    mine = jnp.full((8, 128), -1, I32)
+    for q in range(Q_DEV):
+        for n in range(CAND):
+            row = owner_of[bounded(ids[q, n], OWNERS * PASS_DEV - 1)]
+            mine = jnp.where(lane == CAND * q + n, row, mine)
+    rows_buf[me] = mine
+    pl.semaphore_wait(barrier, len(peers))
+    weights = Gather(place, full_ref, w_send, w_recv)
+    weights.start()
+    rows = Gather(place, rows_buf, r_send, r_recv)
+    rows.start()
+
+    cache_in.wait()
+    cache_f[0 : PLEN * PASS_DEV, :] = cache_ref[...].reshape(PLEN * PASS_DEV, DIM).astype(F32)
+    for r in range(PASS_DEV):
+        tiles[r, ROWS - 16 : ROWS] = jnp.zeros((16, DIM), BF16)
+        tiles[r, 0:PLEN] = cache_f[pl.ds(r, PLEN, stride=PASS_DEV), :].astype(BF16)
     logs[...] = jnp.zeros_like(logs)
     recips[...] = jnp.zeros_like(recips)
 
-    def bounded(value, most):
-        return jnp.minimum(jnp.maximum(value, 0), most)
+    hidden_in.wait()
+    weights.finish()
+    raw = dot(hidden_ref[...], full_ref[...].reshape(-1, DIM))
+    inverse = lax.rsqrt(jnp.mean(raw * raw, axis=-1, keepdims=True) + EPS)
+    vectors = (raw * inverse).astype(BF16)
+    query_ref[me] = vectors.reshape(Q_DEV, QL, DIM)
+    queries = Gather(place, query_ref, q_send, q_recv)
+    queries.start()
+
+    rows.finish()
+    for d in range(OWNERS):
+        rows_vec[d : d + 1, :] = rows_buf[d, 0:1, :]
+    to_rows = pltpu.make_async_copy(rows_vec, rows_tab, tab_sem.at[0])
+    to_rows.start()
+    to_rows.wait()
+    first_row = PASS_DEV * me
+
+    def count_pairs(d, counts):
+        for n in range(PAIRS):
+            counts = counts + jnp.where(lane == rows_tab[d, n] - first_row, 1, 0)
+        return counts
+
+    count_vec[...] = lax.fori_loop(0, OWNERS, count_pairs, jnp.zeros((8, 128), I32))
+    to_count = pltpu.make_async_copy(count_vec, count_tab, tab_sem.at[1])
+    to_count.start()
+    queries.relay(2)
+    to_count.wait()
+    starts = [0]
+    for r in range(PASS_DEV):
+        number = count_tab[0, r]
+        starts.append(starts[-1] + ((number + 3) >> 2))
+        last_tab[r] = jnp.where(number > 0, starts[-1] - 1, -1)
+    slot = iota((8, 128), 0) * 128 + lane
+    group = slot & 63
+    slot_row = jnp.zeros((8, 128), I32)
+    for r in range(1, PASS_DEV):
+        slot_row = slot_row + jnp.where(group >= starts[r], 1, 0)
+    slot_start = jnp.zeros((8, 128), I32)
+    for r in range(1, PASS_DEV):
+        slot_start = jnp.where(slot_row == r, starts[r], slot_start)
+    slot_rank = 4 * (group - slot_start) + (slot >> 6)
+
+    def place_pairs(d, carry):
+        seen, at_slot, at_entry = carry
+        entry = CAND * d
+        for n in range(PAIRS):
+            row = rows_tab[d, n] - first_row
+            pair = PAIRS * d + n
+            same = slot_row == row
+            at_slot = jnp.where(same & (slot_rank == seen), pair, at_slot)
+            seen = seen + jnp.where(same, 1, 0)
+            own = (row >= 0) & (row < PASS_DEV)
+            at_entry = jnp.where(slot == jnp.where(own, entry, -1), pair, at_entry)
+            entry = entry + jnp.where(own, 1, 0)
+        return seen, at_slot, at_entry
+
+    none = jnp.full((8, 128), -1, I32)
+    _, at_slot, at_entry = lax.fori_loop(
+        0, OWNERS, place_pairs, (jnp.zeros((8, 128), I32), none, none - 1)
+    )
+    tab_vec[0] = at_slot
+    tab_vec[1] = slot_row
+    tab_vec[2] = at_entry
+    to_tab = pltpu.make_async_copy(tab_vec.at[pl.ds(0, 3)], tab.at[pl.ds(0, 3)], tab_sem.at[2])
+    to_tab.start()
+    queries.relay(6)
+    to_tab.wait()
+
+    def place_entries(i, spots):
+        for u in range(16):
+            s = 16 * i + u
+            pair = tab[0, s // 128, lax.rem(s, 128)]
+            spots = jnp.where(at_entry == pair, 4 * lax.rem(s, 64) + s // 64, spots)
+        return spots
+
+    tab_vec[3] = lax.fori_loop(0, SLOTS // 16, place_entries, jnp.zeros((8, 128), I32))
+    to_spots = pltpu.make_async_copy(tab_vec.at[3], tab.at[3], tab_sem.at[3])
+    to_spots.start()
+    queries.finish()
+    to_spots.wait()
 
     def row_of(g):
-        return bounded(tab[1, g], PASS_DEV - 1)
+        return bounded(tab[1, 0, g], PASS_DEV - 1)
 
     def load_queries(g):
         parts = []
         for j in range(4):
-            n = bounded(tab[0, 64 * j + g], OWNERS * Q_DEV - 1)
-            parts.append(query_ref[n])
+            pair = tab[0, j // 2, 64 * (j % 2) + g]
+            query = bounded(pair >> 4, OWNERS * Q_DEV - 1)
+            parts.append(query_ref[query >> 2, query & (Q_DEV - 1)])
         return jnp.concatenate(parts, axis=0)
 
     live = iota((ROWS, 128), 0)
@@ -352,14 +331,14 @@
     spread = jnp.where(of_place, jnp.concatenate([logs[...]] * 4, axis=0), 0.0)
     one8 = jnp.ones((8, 128), BF16)
     score_row = TAU * sum(dot_nt(one8, part) for part in pieces(spread))
-    cands = tab_vec[6:7, :]
-    is_cand = ind(iota((CAND, SLOTS), 0) == cands)
-    hits = hit_ref[...]
+    pair = jnp.concatenate([at_slot[0:1], at_slot[1:2]], axis=1)
+    is_cand = ind((iota((CAND, SLOTS), 0) == (pair & (CAND - 1))) & (pair >= 0))
+    lane_of = ((pair >> 6) << 3) + ((pair >> 4) & (Q_DEV - 1))
+    hits = ind((iota((128, SLOTS), 0) == lane_of) & (pair >= 0), BF16)
     mine = sum(
-        dot((is_cand * part[0:1].astype(F32)).astype(BF16), hits) for part in pieces(score_row)
+        dot_nt((is_cand * part[0:1].astype(F32)).astype(BF16), hits) for part in pieces(score_row)
     )
     score_buf[me] = mine[0:8] + pltpu.roll(mine[8:16], 4, 1)
-    pl.semaphore_wait(barrier, len(peers))
     score_swap = Swap(OWNERS, me, lambda t: {"passage": t}, s_send, s_recv)
     score_swap.start(lambda t: score_buf.at[me], score_buf)
 
@@ -376,7 +355,6 @@
     scores = score_buf[0]
     for d in range(1, OWNERS):
         scores = scores + score_buf[d]
-    lane = iota((8, 128), 1)
     low = lax.rem(lane, 8) < Q_DEV
 
     def both(x, op):
@@ -389,46 +367,42 @@
     grad = jnp.concatenate(
         [jnp.where(low, grad, 0.0), jnp.where(low, pltpu.roll(grad, 124, 1), 0.0)], axis=0
     )
-    at_slot = is_cand * sum(dot_nt(part, hits) for part in pieces(grad))
-    at_slot = jnp.sum(at_slot, axis=0, keepdims=True)
-    grad_vec[...] = jnp.broadcast_to(at_slot * root_scale, (8, SLOTS))
+    grad_row = is_cand * sum(dot(part, hits) for part in pieces(grad))
+    grad_row = jnp.sum(grad_row, axis=0, keepdims=True)
+    grad_vec[...] = jnp.broadcast_to(grad_row * root_scale, (8, SLOTS))
     grad_copy = pltpu.make_async_copy(grad_vec, grad_tab, grad_sem)
     grad_copy.start()
     same_group = ind(lax.rem(iota((64, SLOTS), 1), 64) == iota((64, SLOTS), 0))
     to_lanes = ind(of_place, BF16)
-    by_lane = sum(dot(part, to_lanes) for part in pieces(same_group * at_slot))
+    by_lane = sum(dot(part, to_lanes) for part in pieces(same_group * grad_row))
     scales[...] = by_lane * recips[...] * root_scale
     grad_copy.wait()
 
-    def entry_step(i, run):
-        for u in range(4):
-            e = 4 * i + u
-            at = bounded(tab[2, e], 4 * GROUPS - 1)
-            group, spot = at // 4, lax.rem(at, 4)
-            again = (tab[3, e] == tab[3, jnp.maximum(e - 1, 0)]) & (e > 0)
-            run = jnp.where(again, run, 0.0) + qg_group[group, spot] * grad_tab[0, 64 * spot + group]
-            qg_run[e] = run
-        return run
-
-    lax.fori_loop(0, ENTRIES // 4, entry_step, jnp.zeros((QL, DIM), F32))
-
-    def finish_query(d, _):
+    def sum_device(d, _):
+        sums = [jnp.zeros((QL, DIM), F32) for _ in range(Q_DEV)]
+        for n in range(CAP):
+            sub, spot_lane = d // 8, CAND * lax.rem(d, 8) + n
+            pair = tab[2, sub, spot_lane]
+            at = bounded(tab[3, sub, spot_lane], 4 * GROUPS - 1)
+            part = qg_group[at >> 2, at & 3]
+            grad = grad_tab[0, 64 * (at & 3) + (at >> 2)]
+            for q in range(Q_DEV):
+                one = jnp.where((pair >= 0) & (((pair >> 4) & (Q_DEV - 1)) == q), grad, 0.0)
+                sums[q] = sums[q] + part * one
         for q in range(Q_DEV):
-            last = tab[5, 8 * d + q]
-            value = jnp.where(last >= 0, qg_run[bounded(last, ENTRIES - 1)], 0.0)
-            qg_ref[d // NC, lax.rem(d, NC), q * QL : (q + 1) * QL, :] = value.astype(BF16)
+            qg_ref[d // NC, lax.rem(d, NC), q * QL : (q + 1) * QL, :] = sums[q].astype(BF16)
         return 0
 
-    lax.fori_loop(0, OWNERS, finish_query, 0)
+    lax.fori_loop(0, OWNERS, sum_device, 0)
     q_pair = remote(qg_ref.at[:, 1 - c], q_sib, qs_send, qs_recv, sibling)
     q_pair.start()
 
     def cache_step(i, run):
         for u in range(4):
             g = 4 * i + u
-            row = tab[1, g]
+            row = row_of(g)
             w = (exps[g] * scales[pl.ds(g, 1), :]).astype(BF16)
-            again = (row == tab[1, jnp.maximum(g - 1, 0)]) & (g > 0)
+            again = (row == row_of(jnp.maximum(g - 1, 0))) & (g > 0)
             cg_run[g + 1] = jnp.where(again, cg_run[g], 0.0) + dot(w, load_queries(g))
         return run
 
@@ -442,7 +416,7 @@
     lax.fori_loop(4, GROUPS // 4, cache_step, 0)
 
     for r in range(PASS_DEV):
-        last = tab[4, r]
+        last = last_tab[r]
         value = jnp.where(last >= 0, cg_run[bounded(last, GROUPS - 1) + 1], 0.0)
         cache_f[pl.ds(r, ROWS, stride=PASS_DEV), :] = value
     cg_ref[...] = cache_f[...].astype(BF16)
@@ -475,7 +449,6 @@
     query_gradient = q_out[z].astype(F32)
     for k in range(1, NZ):
         query_gradient = query_gradient + q_in[lax.rem(z + k, NZ)].astype(F32)
-    raw = raw_ref[...]
     inverse = lax.rsqrt(jnp.mean(raw * raw, axis=-1, keepdims=True) + EPS)
     mean_term = jnp.mean(query_gradient * raw, axis=-1, keepdims=True)
     raw_grad = (
@@ -587,12 +560,31 @@
 
     q_pair.wait_send()
     w_pair.wait_send()
-    for moved in (score_swap, q_swap, w_swap, x_swap, y_swap):
+    for moved in (weights, rows, queries, score_swap, q_swap, w_swap, x_swap, y_swap):
         moved.drain()
     for copy in sent:
         copy.wait_send()
     b_out.wait()
     a_out.wait()
+
+
+def result_kernel(hid, wg, cache, hid_out, wg_out, cache_out, hid_buf, wg_buf, cache_buf, sems):
+    part = PLEN * PASS_DEV // 4
+    moves = []
+    for n in range(4):
+        span = pl.ds(n * part, part)
+        moves.append((cache.at[span, :], cache_buf.at[span, :], cache_out.at[span, :]))
+    moves += [(hid, hid_buf, hid_out), (wg, wg_buf, wg_out)]
+    reads, writes = [], []
+    for n, (src, mid, _) in enumerate(moves):
+        reads.append(pltpu.make_async_copy(src, mid, sems.at[0, n]))
+        reads[-1].start()
+    for n, (_, mid, dst) in enumerate(moves):
+        reads[n].wait()
+        writes.append(pltpu.make_async_copy(mid, dst, sems.at[1, n]))
+        writes[-1].start()
+    for copy in writes:
+        copy.wait()
 
 
 VMEM = pl.BlockSpec(memory_space=pltpu.VMEM)
@@ -624,25 +616,20 @@
     def pair(*sizes):
         return [dma(sizes), dma(sizes)]
 
-    gather = [dma((2 * NZ - 1,)), dma((OWNERS,))]
-    hidden = hidden.reshape(tokens, width)
-    queries, full, raw, tab, hits, tiles = call(
-        gather_kernel,
-        0,
-        [
-            shape((OWNERS, tokens, DIM), BF16),
-            shape((OWNERS, share, DIM), BF16),
-            shape((tokens, DIM), F32),
-            shape((8, SLOTS), I32),
-            shape((SLOTS, 128), BF16),
-            shape((PASS_DEV, ROWS, DIM), BF16),
-        ],
-        [VMEM] * 5,
-        [VMEM] * 6,
-        [vmem((OWNERS, 8, 128), F32), vmem((PLEN * PASS_DEV, DIM), F32)] + gather + gather + gather,
-        (hidden, weight, jnp.transpose(cache, (1, 0, 2)), passage_ids, owner_map.reshape(1, -1)),
-    )
     scratch = [
+        vmem((tokens, width), BF16),
+        vmem((PLEN, PASS_DEV, DIM), BF16),
+        vmem((OWNERS, Q_DEV, QL, DIM), BF16),
+        vmem((OWNERS, share, DIM), BF16),
+        vmem((PASS_DEV, ROWS, DIM), BF16),
+        vmem((OWNERS, 8, 128), I32),
+        vmem((OWNERS, 128), I32),
+        pltpu.SMEM((OWNERS, 128), I32),
+        vmem((8, 128), I32),
+        pltpu.SMEM((8, 128), I32),
+        vmem((4, 8, 128), I32),
+        pltpu.SMEM((4, 8, 128), I32),
+        pltpu.SMEM((PASS_DEV,), I32),
         vmem((FLAT, DIM), F32),
         vmem((GROUPS, ROWS, 128), F32),
         vmem((64, 128), F32),
@@ -653,7 +640,6 @@
         pltpu.SMEM((8, SLOTS), F32),
         vmem((GROUPS + 1, ROWS, DIM), F32),
         vmem((GROUPS, 4, QL, DIM), F32),
-        vmem((ENTRIES, QL, DIM), F32),
         vmem((NZ, NC, tokens, DIM), BF16),
         vmem((FLAT, DIM), BF16),
         vmem((NX - 1, NY, A_ROWS, DIM), BF16),
@@ -672,28 +658,45 @@
         vmem((NZ, share, DIM), BF16),
         vmem((NX, share, DIM), BF16),
         vmem((NY, share, DIM), BF16),
+        dma((2,)),
+        dma((4,)),
         dma,
         dma((2,)),
     ]
+    gather = [dma((2 * NZ - 1,)), dma((OWNERS,))]
     swap = lambda n: [dma((n - 1,)), dma((n,))]
-    scratch += swap(OWNERS)
+    scratch += gather + gather + gather + swap(OWNERS)
     scratch += [dma, dma] + swap(NZ) + [dma, dma] + swap(NZ) + swap(NX) + swap(NY)
     scratch += pair(NX - 1, NY) + pair(NY - 1) + pair(NY - 1) + pair(NX - 1, NY)
     scratch += pair(NY - 1) + pair(NX - 1) + pair(NX - 1) + pair(NY - 1)
 
     hid, wg, cache_grad = call(
         pair_kernel,
-        1,
+        0,
         [
             shape((tokens, width), BF16),
             shape((share, DIM), F32),
             shape((PLEN * PASS_DEV, DIM), BF16),
         ],
-        [VMEM, VMEM, VMEM, VMEM, SMEM, SMEM, VMEM, VMEM, VMEM],
+        [ANY, VMEM, ANY, SMEM, SMEM, SMEM],
         [VMEM, VMEM, ANY],
         scratch,
-        (hidden, full, raw, tiles, lengths, tab, tab, hits, queries.reshape(OWNERS * Q_DEV, QL, DIM)),
+        (
+            hidden.reshape(tokens, width),
+            weight,
+            jnp.transpose(cache, (1, 0, 2)),
+            lengths,
+            passage_ids,
+            owner_map,
+        ),
     )
+    hid, wg, cache_grad = pl.pallas_call(
+        result_kernel,
+        out_shape=[shape(x.shape, x.dtype) for x in (hid, wg, cache_grad)],
+        in_specs=[ANY] * 3,
+        out_specs=[ANY] * 3,
+        scratch_shapes=[vmem(x.shape, x.dtype) for x in (hid, wg, cache_grad)] + [dma((2, 6))],
+    )(hid, wg, cache_grad)
     cache_grad = jnp.transpose(cache_grad.reshape(PLEN, PASS_DEV, DIM), (1, 0, 2))
     return hid.reshape(Q_DEV, QL, width), wg, cache_grad
 

time: 89 us -> 88.6 us (level); the launches traced: 87.3 us -> 88.4 us
  Pallas kernels: 82.3 us -> 87.8 us
  local copies, waits for them, and re-layouts: 4.34 us -> 0 us
    unnamed x5 -> x0, local copies, waits for them, and re-layouts: 4.34 us -> none
    pallas_call x2 -> x1, Pallas kernels: 82.3 us -> 85.7 us  [call(): pl.pallas_call(kernel, out_shape=out_shape, in_specs=in_specs, out_specs=...]
    pallas_call x0 -> x1, Pallas kernels: none -> 2.04 us  [shards(): pl.pallas_call(result_kernel, out_shape=[shape(x.shape, x.dtype) for x in...]
where the time goes in v4:
time: 88.6 us; the launch traced here: 88.4 us
  Pallas kernels  87.8 us (99%)
    pallas_call x1, Pallas kernels, call(): pl.pallas_call(kernel, out_shape=out_shape, in_specs=in_specs, out_specs=...  85.7 us
    pallas_call x1, Pallas kernels, shards(): pl.pallas_call(result_kernel, out_shape=[shape(x.shape, x.dtype) for x in...  2.04 us

profile of v4, /device:TPU:1, one launch (start us, length us, event | category | flops | bytes accessed | tf_op | source)
XLA Modules:
  0.0 88.4 jit_solution(2188085320034835436)
XLA Ops:
  0.6 85.7 %shard_map.85 = (bf16[128,768]{1,0:T(8,128)(2,1)}, f32[48,128]{1,0:T(8,128)}, bf16[2880,128]{1,0:T(8,128)(2,1)}) custom-call(bf16[128,768]{1,0:T(8,128)(2,1)} %bitcast.7, bf16[48,128]{1,0:T(8,128)(2,1)} %weight_ref.1, bf16[180,16,128]{2,1,0:T(8,128)(2,1)} %bitcast.6, s32[16]{0:T(128)} %len_ref.1, s32[4,16]{1,0:T(4,128)} %ids.1, s32[256]{0:T(256)} %owner_of.1), custom_call_target="tpu_custom_call" | custom-call | tf_op jit(solution)/shard_map/pallas_call | solution.py:596
  86.4 2.0 %shard_map.86 = (bf16[128,768]{1,0:T(8,128)(2,1)}, f32[48,128]{1,0:T(8,128)}, bf16[2880,128]{1,0:T(8,128)(2,1)}) custom-call(bf16[128,768]{1,0:T(8,128)(2,1)} %get-tuple-element.9.hid, f32[48,128]{1,0:T(8,128)} %get-tuple-element.10.wg, bf16[2880,128]{1,0:T(8,128)(2,1)} %get-tuple-element.11.cache), custom_call_target="tpu_custom_call" | custom-call | tf_op jit(solution)/shard_map/pallas_call | solution.py:693

commit v5 on v4

--- a/solution.py
+++ b/solution.py
@@ -55,14 +55,14 @@
 class Place:
     def __init__(self):
         self.me = lax.axis_index("passage")
-        self.z, self.c = self.me // NC, lax.rem(self.me, NC)
+        self.z, self.c = self.me >> 1, self.me & (NC - 1)
         self.sibling = self.z * NC + (1 - self.c)
 
     def ring(self, k):
-        return lax.rem(self.z + k, NZ) * NC + self.c
+        return ((self.z + k) & (NZ - 1)) * NC + self.c
 
     def ring_sibling(self, k):
-        return lax.rem(self.z + k, NZ) * NC + (1 - self.c)
+        return ((self.z + k) & (NZ - 1)) * NC + (1 - self.c)
 
 
 def remote(src, dst, send, recv, device):
@@ -138,7 +138,7 @@
         self.buf, self.copies = buf, []
         far = sorted(range(1, self.n), key=lambda k: -min(k, self.n - k))
         for k in far:
-            t = lax.rem(self.at + k, self.n)
+            t = (self.at + k) & (self.n - 1)
             copy = remote(
                 src_of(t), buf.at[self.at], self.send.at[k - 1], self.recv.at[self.at], self.device(t)
             )
@@ -147,7 +147,7 @@
 
     def finish(self):
         for k in range(1, self.n):
-            t = lax.rem(self.at + k, self.n)
+            t = (self.at + k) & (self.n - 1)
             remote(
                 self.buf.at[t], self.buf.at[t], self.send.at[0], self.recv.at[t], self.device(t)
             ).wait_recv()
@@ -160,8 +160,8 @@
 def pair_kernel(
     hidden_hbm, weight_ref, cache_hbm, len_ref, ids, owner_of,
     hid_ref, wg_ref, cache_out,
-    hidden_ref, cache_ref, query_ref, full_ref, tiles, rows_buf, rows_vec, rows_tab, count_vec, count_tab,
-    tab_vec, tab, last_tab,
+    hidden_ref, cache_ref, query_ref, full_ref, tiles, rows_buf, rows_vec, rows_tab,
+    tab_vec, tab,
     cache_f, exps, logs, recips, scales,
     score_buf, grad_vec, grad_tab, cg_run, qg_group, qg_ref, cg_ref,
     ax_buf, ay_buf, by_buf, bx_buf, mid_a, mid_b, fin, q_sib, q_out, q_in, w_own, w_sib, w_out, w_in, w_x, w_y,
@@ -174,10 +174,10 @@
     place = Place()
     me, z, c = place.me, place.z, place.c
     dp = lax.axis_index("dp")
-    ix, iy = dp // NY, lax.rem(dp, NY)
-    others = [lax.rem(me + k, OWNERS) for k in range(1, OWNERS)]
-    to_x = lambda k: {"dp": lax.rem(ix + k, NX) * NY + iy}
-    to_y = lambda k: {"dp": ix * NY + lax.rem(iy + k, NY)}
+    ix, iy = dp >> 3, dp & (NY - 1)
+    others = [(me + k) & (OWNERS - 1) for k in range(1, OWNERS)]
+    to_x = lambda k: {"dp": ((ix + k) & (NX - 1)) * NY + iy}
+    to_y = lambda k: {"dp": ix * NY + ((iy + k) & (NY - 1))}
     sibling = {"passage": place.sibling}
     similarity_scale = 1.0 / (TAU * math.sqrt(DIM))
     root_scale = 1.0 / math.sqrt(DIM)
@@ -197,11 +197,14 @@
 
     full_ref[me] = weight_ref[...]
     lane = iota((8, 128), 1)
+    slot = iota((8, 128), 0) * 128 + lane
     mine = jnp.full((8, 128), -1, I32)
-    for q in range(Q_DEV):
-        for n in range(CAND):
-            row = owner_of[bounded(ids[q, n], OWNERS * PASS_DEV - 1)]
-            mine = jnp.where(lane == CAND * q + n, row, mine)
+    listed = jnp.zeros((8, 128), I32)
+    for n in range(PAIRS):
+        row = owner_of[bounded(ids[n // CAND, n % CAND], OWNERS * PASS_DEV - 1)]
+        same = (slot >> 4) == (row >> 4)
+        mine = jnp.where(same & ((slot & 15) == listed), 256 * n + row, mine)
+        listed = listed + jnp.where(same, 1, 0)
     rows_buf[me] = mine
     pl.semaphore_wait(barrier, len(peers))
     weights = Gather(place, full_ref, w_send, w_recv)
@@ -217,6 +220,12 @@
     logs[...] = jnp.zeros_like(logs)
     recips[...] = jnp.zeros_like(recips)
 
+    weights.relay(NZ - 1)
+    rows.finish()
+    for d in range(OWNERS):
+        rows_vec[d : d + 1, :] = rows_buf[d, pl.ds(me >> 3, 1), :]
+    to_rows = pltpu.make_async_copy(rows_vec, rows_tab, tab_sem.at[0])
+    to_rows.start()
     hidden_in.wait()
     weights.finish()
     raw = dot(hidden_ref[...], full_ref[...].reshape(-1, DIM))
@@ -226,51 +235,44 @@
     queries = Gather(place, query_ref, q_send, q_recv)
     queries.start()
 
-    rows.finish()
-    for d in range(OWNERS):
-        rows_vec[d : d + 1, :] = rows_buf[d, 0:1, :]
-    to_rows = pltpu.make_async_copy(rows_vec, rows_tab, tab_sem.at[0])
-    to_rows.start()
     to_rows.wait()
     first_row = PASS_DEV * me
 
+    my_lane = 16 * (me & 7)
+
+    def listed_pair(d, n):
+        value = rows_tab[d, my_lane + n]
+        row = jnp.where(value >= 0, (value & 255) - first_row, -1)
+        return jnp.where(value >= 0, PAIRS * d + (value >> 8), -1), row
+
+    deep = iota((PASS_DEV, 128), 0)
+
     def count_pairs(d, counts):
-        for n in range(PAIRS):
-            counts = counts + jnp.where(lane == rows_tab[d, n] - first_row, 1, 0)
+        for n in range(CAP):
+            counts = counts + jnp.where(deep == listed_pair(d, n)[1], 1, 0)
         return counts
 
-    count_vec[...] = lax.fori_loop(0, OWNERS, count_pairs, jnp.zeros((8, 128), I32))
-    to_count = pltpu.make_async_copy(count_vec, count_tab, tab_sem.at[1])
-    to_count.start()
-    queries.relay(2)
-    to_count.wait()
-    starts = [0]
+    counts = lax.fori_loop(0, OWNERS, count_pairs, jnp.zeros((PASS_DEV, 128), I32))
+    group = slot & 63
+    start = jnp.zeros((8, 128), I32)
+    slot_row, slot_start, last = start, start, start - 1
     for r in range(PASS_DEV):
-        number = count_tab[0, r]
-        starts.append(starts[-1] + ((number + 3) >> 2))
-        last_tab[r] = jnp.where(number > 0, starts[-1] - 1, -1)
-    slot = iota((8, 128), 0) * 128 + lane
-    group = slot & 63
-    slot_row = jnp.zeros((8, 128), I32)
-    for r in range(1, PASS_DEV):
-        slot_row = slot_row + jnp.where(group >= starts[r], 1, 0)
-    slot_start = jnp.zeros((8, 128), I32)
-    for r in range(1, PASS_DEV):
-        slot_start = jnp.where(slot_row == r, starts[r], slot_start)
+        number = jnp.broadcast_to(counts[r : r + 1, :], (8, 128))
+        if r:
+            slot_row = slot_row + jnp.where(group >= start, 1, 0)
+            slot_start = jnp.where(group >= start, start, slot_start)
+        start = start + ((number + 3) >> 2)
+        last = jnp.where((lane == r) & (number > 0), start - 1, last)
     slot_rank = 4 * (group - slot_start) + (slot >> 6)
 
     def place_pairs(d, carry):
         seen, at_slot, at_entry = carry
-        entry = CAND * d
-        for n in range(PAIRS):
-            row = rows_tab[d, n] - first_row
-            pair = PAIRS * d + n
+        for n in range(CAP):
+            pair, row = listed_pair(d, n)
             same = slot_row == row
             at_slot = jnp.where(same & (slot_rank == seen), pair, at_slot)
             seen = seen + jnp.where(same, 1, 0)
-            own = (row >= 0) & (row < PASS_DEV)
-            at_entry = jnp.where(slot == jnp.where(own, entry, -1), pair, at_entry)
-            entry = entry + jnp.where(own, 1, 0)
+            at_entry = jnp.where((slot == 16 * d + n) & (pair >= 0), pair, at_entry)
         return seen, at_slot, at_entry
 
     none = jnp.full((8, 128), -1, I32)
@@ -280,23 +282,11 @@
     tab_vec[0] = at_slot
     tab_vec[1] = slot_row
     tab_vec[2] = at_entry
-    to_tab = pltpu.make_async_copy(tab_vec.at[pl.ds(0, 3)], tab.at[pl.ds(0, 3)], tab_sem.at[2])
+    tab_vec[3] = last
+    to_tab = pltpu.make_async_copy(tab_vec.at[pl.ds(0, 4)], tab.at[pl.ds(0, 4)], tab_sem.at[1])
     to_tab.start()
-    queries.relay(6)
+    queries.finish()
     to_tab.wait()
-
-    def place_entries(i, spots):
-        for u in range(16):
-            s = 16 * i + u
-            pair = tab[0, s // 128, lax.rem(s, 128)]
-            spots = jnp.where(at_entry == pair, 4 * lax.rem(s, 64) + s // 64, spots)
-        return spots
-
-    tab_vec[3] = lax.fori_loop(0, SLOTS // 16, place_entries, jnp.zeros((8, 128), I32))
-    to_spots = pltpu.make_async_copy(tab_vec.at[3], tab.at[3], tab_sem.at[3])
-    to_spots.start()
-    queries.finish()
-    to_spots.wait()
 
     def row_of(g):
         return bounded(tab[1, 0, g], PASS_DEV - 1)
@@ -341,6 +331,16 @@
     score_buf[me] = mine[0:8] + pltpu.roll(mine[8:16], 4, 1)
     score_swap = Swap(OWNERS, me, lambda t: {"passage": t}, s_send, s_recv)
     score_swap.start(lambda t: score_buf.at[me], score_buf)
+
+    def place_entries(i, spots):
+        for u in range(16):
+            pair = tab[0, i >> 3, 16 * (i & 7) + u]
+            spots = jnp.where(at_entry == pair, 64 * (i & 3) + (i >> 2) + 4 * u, spots)
+        return spots
+
+    tab_vec[4] = lax.fori_loop(0, SLOTS // 16, place_entries, jnp.zeros((8, 128), I32))
+    to_spots = pltpu.make_async_copy(tab_vec.at[4], tab.at[4], tab_sem.at[2])
+    to_spots.start()
 
     def products(i, _):
         for u in range(4):
@@ -376,21 +376,22 @@
     to_lanes = ind(of_place, BF16)
     by_lane = sum(dot(part, to_lanes) for part in pieces(same_group * grad_row))
     scales[...] = by_lane * recips[...] * root_scale
+    to_spots.wait()
     grad_copy.wait()
 
     def sum_device(d, _):
         sums = [jnp.zeros((QL, DIM), F32) for _ in range(Q_DEV)]
         for n in range(CAP):
-            sub, spot_lane = d // 8, CAND * lax.rem(d, 8) + n
+            sub, spot_lane = d >> 3, 16 * (d & 7) + n
             pair = tab[2, sub, spot_lane]
-            at = bounded(tab[3, sub, spot_lane], 4 * GROUPS - 1)
+            at = bounded(tab[4, sub, spot_lane], 4 * GROUPS - 1)
             part = qg_group[at >> 2, at & 3]
             grad = grad_tab[0, 64 * (at & 3) + (at >> 2)]
             for q in range(Q_DEV):
                 one = jnp.where((pair >= 0) & (((pair >> 4) & (Q_DEV - 1)) == q), grad, 0.0)
                 sums[q] = sums[q] + part * one
         for q in range(Q_DEV):
-            qg_ref[d // NC, lax.rem(d, NC), q * QL : (q + 1) * QL, :] = sums[q].astype(BF16)
+            qg_ref[d >> 1, d & 1, q * QL : (q + 1) * QL, :] = sums[q].astype(BF16)
         return 0
 
     lax.fori_loop(0, OWNERS, sum_device, 0)
@@ -416,7 +417,7 @@
     lax.fori_loop(4, GROUPS // 4, cache_step, 0)
 
     for r in range(PASS_DEV):
-        last = last_tab[r]
+        last = tab[3, 0, r]
         value = jnp.where(last >= 0, cg_run[bounded(last, GROUPS - 1) + 1], 0.0)
         cache_f[pl.ds(r, ROWS, stride=PASS_DEV), :] = value
     cg_ref[...] = cache_f[...].astype(BF16)
@@ -432,10 +433,10 @@
         remote(dst, dst, send, recv, sibling).wait_recv()
 
     def y_at(k):
-        return lax.rem(iy + k + NY, NY)
+        return (iy + k) & (NY - 1)
 
     def x_at(k):
-        return lax.rem(ix + k + NX, NX)
+        return (ix + k) & (NX - 1)
 
     for k in FAR:
         src = cg_ref.at[rows_at(B_AT + y_at(k) * B_PIECE, B_PIECE), :]
@@ -448,7 +449,7 @@
     q_swap.finish()
     query_gradient = q_out[z].astype(F32)
     for k in range(1, NZ):
-        query_gradient = query_gradient + q_in[lax.rem(z + k, NZ)].astype(F32)
+        query_gradient = query_gradient + q_in[(z + k) & (NZ - 1)].astype(F32)
     inverse = lax.rsqrt(jnp.mean(raw * raw, axis=-1, keepdims=True) + EPS)
     mean_term = jnp.mean(query_gradient * raw, axis=-1, keepdims=True)
     raw_grad = (
@@ -510,7 +511,7 @@
     w_swap.finish()
     total = w_out[z].astype(F32)
     for k in range(1, NZ):
-        total = total + w_in[lax.rem(z + k, NZ)].astype(F32)
+        total = total + w_in[(z + k) & (NZ - 1)].astype(F32)
     w_x[ix] = total.astype(BF16)
     x_swap = Swap(NX, ix, lambda t: {"dp": t * NY + iy}, wx_send, wx_recv)
     x_swap.start(lambda t: w_x.at[ix], w_x)
@@ -625,11 +626,8 @@
         vmem((OWNERS, 8, 128), I32),
         vmem((OWNERS, 128), I32),
         pltpu.SMEM((OWNERS, 128), I32),
-        vmem((8, 128), I32),
-        pltpu.SMEM((8, 128), I32),
-        vmem((4, 8, 128), I32),
-        pltpu.SMEM((4, 8, 128), I32),
-        pltpu.SMEM((PASS_DEV,), I32),
+        vmem((5, 8, 128), I32),
+        pltpu.SMEM((5, 8, 128), I32),
         vmem((FLAT, DIM), F32),
         vmem((GROUPS, ROWS, 128), F32),
         vmem((64, 128), F32),

time: 88.6 us -> 83.1 us (0.938)
  Pallas kernels: 87.8 us -> 82.1 us
    pallas_call x1, Pallas kernels: 85.7 us -> 80.1 us  [call(): pl.pallas_call(kernel, out_shape=out_shape, in_specs=in_specs, out_specs=...]
where the time goes in v5:
time: 83.1 us; the launch traced here: 82.8 us
  Pallas kernels  82.1 us (99%)
    pallas_call x1, Pallas kernels, call(): pl.pallas_call(kernel, out_shape=out_shape, in_specs=in_specs, out_specs=...  80.1 us
    pallas_call x1, Pallas kernels, shards(): pl.pallas_call(result_kernel, out_shape=[shape(x.shape, x.dtype) for x in...  2.04 us

profile of v5, /device:TPU:1, one launch (start us, length us, event | category | flops | bytes accessed | tf_op | source)
XLA Modules:
  0.0 82.8 jit_solution(9063105081141554089)
XLA Ops:
  0.6 80.1 %shard_map.85 = (bf16[128,768]{1,0:T(8,128)(2,1)}, f32[48,128]{1,0:T(8,128)}, bf16[2880,128]{1,0:T(8,128)(2,1)}) custom-call(bf16[128,768]{1,0:T(8,128)(2,1)} %bitcast.7, bf16[48,128]{1,0:T(8,128)(2,1)} %weight_ref.1, bf16[180,16,128]{2,1,0:T(8,128)(2,1)} %bitcast.6, s32[16]{0:T(128)} %len_ref.1, s32[4,16]{1,0:T(4,128)} %ids.1, s32[256]{0:T(256)} %owner_of.1), custom_call_target="tpu_custom_call" | custom-call | tf_op jit(solution)/shard_map/pallas_call | solution.py:597
  80.7 2.0 %shard_map.86 = (bf16[128,768]{1,0:T(8,128)(2,1)}, f32[48,128]{1,0:T(8,128)}, bf16[2880,128]{1,0:T(8,128)(2,1)}) custom-call(bf16[128,768]{1,0:T(8,128)(2,1)} %get-tuple-element.9.hid, f32[48,128]{1,0:T(8,128)} %get-tuple-element.10.wg, bf16[2880,128]{1,0:T(8,128)(2,1)} %get-tuple-element.11.cache), custom_call_target="tpu_custom_call" | custom-call | tf_op jit(solution)/shard_map/pallas_call | solution.py:691

commit v6 on v5

--- a/solution.py
+++ b/solution.py
@@ -17,6 +17,7 @@
 PASS_DEV, PLEN, ROWS = 16, 180, 192
 DIM = 128
 GROUPS = 60
+UNROLL = 20
 SLOTS = 256
 CAP = 12
 PAIRS = Q_DEV * CAND
@@ -120,7 +121,7 @@
 
 
 FAR = (4, 3, 5, 2, 6, 1, 7)
-A_ROWS, B_ROWS = 64, 32
+A_ROWS, B_ROWS = 80, 16
 A_PIECE, B_PIECE = NY * A_ROWS, NX * B_ROWS
 B_AT = NX * A_PIECE
 FLAT = PASS_DEV * ROWS
@@ -302,8 +303,8 @@
     live = iota((ROWS, 128), 0)
 
     def forward(i, _):
-        for u in range(4):
-            g = 4 * i + u
+        for u in range(UNROLL):
+            g = UNROLL * i + u
             row = row_of(g)
             sims = dot_nt(tiles[row], load_queries(g)) * similarity_scale
             sims = jnp.where(live < len_ref[row], sims, NEG)
@@ -315,7 +316,7 @@
             recips[pl.ds(g, 1), :] = 1.0 / total
         return 0
 
-    lax.fori_loop(0, GROUPS // 4, forward, 0)
+    lax.fori_loop(0, GROUPS // UNROLL, forward, 0)
 
     of_place = iota((SLOTS, 128), 1) // QL == iota((SLOTS, 128), 0) // 64
     spread = jnp.where(of_place, jnp.concatenate([logs[...]] * 4, axis=0), 0.0)
@@ -343,13 +344,13 @@
     to_spots.start()
 
     def products(i, _):
-        for u in range(4):
-            g = 4 * i + u
+        for u in range(UNROLL):
+            g = UNROLL * i + u
             w = (exps[g] * recips[pl.ds(g, 1), :]).astype(BF16)
             qg_group[g] = dot_tn(w, tiles[row_of(g)]).reshape(4, QL, DIM)
         return 0
 
-    lax.fori_loop(0, GROUPS // 4, products, 0)
+    lax.fori_loop(0, GROUPS // UNROLL, products, 0)
 
     score_swap.finish()
     scores = score_buf[0]
@@ -399,22 +400,22 @@
     q_pair.start()
 
     def cache_step(i, run):
-        for u in range(4):
-            g = 4 * i + u
+        for u in range(UNROLL):
+            g = UNROLL * i + u
             row = row_of(g)
             w = (exps[g] * scales[pl.ds(g, 1), :]).astype(BF16)
             again = (row == row_of(jnp.maximum(g - 1, 0))) & (g > 0)
             cg_run[g + 1] = jnp.where(again, cg_run[g], 0.0) + dot(w, load_queries(g))
         return run
 
-    lax.fori_loop(0, 4, cache_step, 0)
+    lax.fori_loop(0, 1, cache_step, 0)
     q_pair.wait_recv()
     for t in range(NZ):
         q_out[t] = (qg_ref[t, c].astype(F32) + q_sib[t].astype(F32)).astype(BF16)
     on_z = lambda t: {"passage": t * NC + c}
     q_swap = Swap(NZ, z, on_z, qz_send, qz_recv)
     q_swap.start(lambda t: q_out.at[t], q_in)
-    lax.fori_loop(4, GROUPS // 4, cache_step, 0)
+    lax.fori_loop(1, GROUPS // UNROLL, cache_step, 0)
 
     for r in range(PASS_DEV):
         last = tab[3, 0, r]
@@ -488,15 +489,6 @@
     for k in (2, 1, 3):
         src = mid_b.at[rows_at(x_at(k) * B_ROWS, B_ROWS), :]
         push(src, bx_buf.at[k - 1], b2_send.at[k - 1], b2_recv.at[k - 1], to_x(k))
-    total = mid_b[rows_at(ix * B_ROWS, B_ROWS), :].astype(F32)
-    for k in range(1, NX):
-        await_recv(bx_buf.at[k - 1], b2_send.at[k - 1], b2_recv.at[k - 1])
-        total = total + bx_buf[k - 1].astype(F32)
-    b_span = lambda kx, ky: fin.at[rows_at(B_AT + y_at(ky) * B_PIECE + x_at(kx) * B_ROWS, B_ROWS), :]
-    fin[rows_at(B_AT + iy * B_PIECE + ix * B_ROWS, B_ROWS), :] = total.astype(BF16)
-    for k in (2, 1, 3):
-        push(b_span(0, 0), b_span(0, 0), b3_send.at[k - 1], b3_recv.at[k - 1], to_x(k))
-
     total = mid_a[0].astype(F32)
     for d in range(1, NY):
         await_recv(ay_buf.at[d - 1], a2_send.at[d - 1], a2_recv.at[d - 1])
@@ -507,6 +499,15 @@
         push(a_span(0, 0), a_span(0, 0), a3_send.at[d - 1], a3_recv.at[d - 1], to_y(d))
     for k in (2, 1, 3):
         push(a_span(0, 0), a_span(0, 0), a4_send.at[k - 1, 0], a4_recv.at[k - 1, 0], to_x(k))
+
+    total = mid_b[rows_at(ix * B_ROWS, B_ROWS), :].astype(F32)
+    for k in range(1, NX):
+        await_recv(bx_buf.at[k - 1], b2_send.at[k - 1], b2_recv.at[k - 1])
+        total = total + bx_buf[k - 1].astype(F32)
+    b_span = lambda kx, ky: fin.at[rows_at(B_AT + y_at(ky) * B_PIECE + x_at(kx) * B_ROWS, B_ROWS), :]
+    fin[rows_at(B_AT + iy * B_PIECE + ix * B_ROWS, B_ROWS), :] = total.astype(BF16)
+    for k in (2, 1, 3):
+        push(b_span(0, 0), b_span(0, 0), b3_send.at[k - 1], b3_recv.at[k - 1], to_x(k))
 
     w_swap.finish()
     total = w_out[z].astype(F32)

time: 83.1 us -> 79.4 us (0.955); the launches traced: 82.8 us -> 78.1 us
  Pallas kernels: 82.1 us -> 77.4 us
    pallas_call x1, Pallas kernels: 80.1 us -> 75.4 us  [call(): pl.pallas_call(kernel, out_shape=out_shape, in_specs=in_specs, out_specs=...]
where the time goes in v6:
time: 79.4 us; the launch traced here: 78.1 us
  Pallas kernels  77.4 us (97%)
    pallas_call x1, Pallas kernels, call(): pl.pallas_call(kernel, out_shape=out_shape, in_specs=in_specs, out_specs=...  75.4 us
    pallas_call x1, Pallas kernels, shards(): pl.pallas_call(result_kernel, out_shape=[shape(x.shape, x.dtype) for x in...  2.04 us

profile of v6, /device:TPU:1, one launch (start us, length us, event | category | flops | bytes accessed | tf_op | source)
XLA Modules:
  0.0 78.1 jit_solution(15210822841166112620)
XLA Ops:
  0.6 75.4 %shard_map.85 = (bf16[128,768]{1,0:T(8,128)(2,1)}, f32[48,128]{1,0:T(8,128)}, bf16[2880,128]{1,0:T(8,128)(2,1)}) custom-call(bf16[128,768]{1,0:T(8,128)(2,1)} %bitcast.7, bf16[48,128]{1,0:T(8,128)(2,1)} %weight_ref.1, bf16[180,16,128]{2,1,0:T(8,128)(2,1)} %bitcast.6, s32[16]{0:T(128)} %len_ref.1, s32[4,16]{1,0:T(4,128)} %ids.1, s32[256]{0:T(256)} %owner_of.1), custom_call_target="tpu_custom_call" | custom-call | tf_op jit(solution)/shard_map/pallas_call | solution.py:598
  76.0 2.0 %shard_map.86 = (bf16[128,768]{1,0:T(8,128)(2,1)}, f32[48,128]{1,0:T(8,128)}, bf16[2880,128]{1,0:T(8,128)(2,1)}) custom-call(bf16[128,768]{1,0:T(8,128)(2,1)} %get-tuple-element.9.hid, f32[48,128]{1,0:T(8,128)} %get-tuple-element.10.wg, bf16[2880,128]{1,0:T(8,128)(2,1)} %get-tuple-element.11.cache), custom_call_target="tpu_custom_call" | custom-call | tf_op jit(solution)/shard_map/pallas_call | solution.py:692

commit v7 on v6

--- a/solution.py
+++ b/solution.py
@@ -17,7 +17,7 @@
 PASS_DEV, PLEN, ROWS = 16, 180, 192
 DIM = 128
 GROUPS = 60
-UNROLL = 20
+UNROLL = 30
 SLOTS = 256
 CAP = 12
 PAIRS = Q_DEV * CAND
@@ -163,7 +163,7 @@
     hid_ref, wg_ref, cache_out,
     hidden_ref, cache_ref, query_ref, full_ref, tiles, rows_buf, rows_vec, rows_tab,
     tab_vec, tab,
-    cache_f, exps, logs, recips, scales,
+    cache_f, exps, probs, logs, recips,
     score_buf, grad_vec, grad_tab, cg_run, qg_group, qg_ref, cg_ref,
     ax_buf, ay_buf, by_buf, bx_buf, mid_a, mid_b, fin, q_sib, q_out, q_in, w_own, w_sib, w_out, w_in, w_x, w_y,
     in_sem, tab_sem, grad_sem, out_sem,
@@ -292,12 +292,15 @@
     def row_of(g):
         return bounded(tab[1, 0, g], PASS_DEV - 1)
 
-    def load_queries(g):
+    def load_queries(g, scaled=False):
         parts = []
         for j in range(4):
             pair = tab[0, j // 2, 64 * (j % 2) + g]
             query = bounded(pair >> 4, OWNERS * Q_DEV - 1)
-            parts.append(query_ref[query >> 2, query & (Q_DEV - 1)])
+            part = query_ref[query >> 2, query & (Q_DEV - 1)]
+            if scaled:
+                part = (part.astype(F32) * grad_tab[0, 64 * j + g]).astype(BF16)
+            parts.append(part)
         return jnp.concatenate(parts, axis=0)
 
     live = iota((ROWS, 128), 0)
@@ -347,6 +350,7 @@
         for u in range(UNROLL):
             g = UNROLL * i + u
             w = (exps[g] * recips[pl.ds(g, 1), :]).astype(BF16)
+            probs[g] = w
             qg_group[g] = dot_tn(w, tiles[row_of(g)]).reshape(4, QL, DIM)
         return 0
 
@@ -373,10 +377,6 @@
     grad_vec[...] = jnp.broadcast_to(grad_row * root_scale, (8, SLOTS))
     grad_copy = pltpu.make_async_copy(grad_vec, grad_tab, grad_sem)
     grad_copy.start()
-    same_group = ind(lax.rem(iota((64, SLOTS), 1), 64) == iota((64, SLOTS), 0))
-    to_lanes = ind(of_place, BF16)
-    by_lane = sum(dot(part, to_lanes) for part in pieces(same_group * grad_row))
-    scales[...] = by_lane * recips[...] * root_scale
     to_spots.wait()
     grad_copy.wait()
 
@@ -403,9 +403,8 @@
         for u in range(UNROLL):
             g = UNROLL * i + u
             row = row_of(g)
-            w = (exps[g] * scales[pl.ds(g, 1), :]).astype(BF16)
             again = (row == row_of(jnp.maximum(g - 1, 0))) & (g > 0)
-            cg_run[g + 1] = jnp.where(again, cg_run[g], 0.0) + dot(w, load_queries(g))
+            cg_run[g + 1] = jnp.where(again, cg_run[g], 0.0) + dot(probs[g], load_queries(g, True))
         return run
 
     lax.fori_loop(0, 1, cache_step, 0)
@@ -421,7 +420,7 @@
         last = tab[3, 0, r]
         value = jnp.where(last >= 0, cg_run[bounded(last, GROUPS - 1) + 1], 0.0)
         cache_f[pl.ds(r, ROWS, stride=PASS_DEV), :] = value
-    cg_ref[...] = cache_f[...].astype(BF16)
+    cg_ref[B_AT:FLAT, :] = cache_f[B_AT:FLAT, :].astype(BF16)
 
     sent = []
 
@@ -444,7 +443,9 @@
         push(src, by_buf.at[k - 1], b1_send.at[k - 1], b1_recv.at[k - 1], to_y(k))
     for d in FAR + (0,):
         for k in (2, 1, 3):
-            src = cg_ref.at[rows_at(x_at(k) * A_PIECE + y_at(d) * A_ROWS, A_ROWS), :]
+            span = rows_at(x_at(k) * A_PIECE + y_at(d) * A_ROWS, A_ROWS)
+            cg_ref[span, :] = cache_f[span, :].astype(BF16)
+            src = cg_ref.at[span, :]
             push(src, ax_buf.at[k - 1, d], a1_send.at[k - 1, d], a1_recv.at[k - 1, d], to_x(k))
 
     q_swap.finish()
@@ -462,7 +463,7 @@
     w_pair.start()
 
     def a_first(d):
-        total = cg_ref[rows_at(ix * A_PIECE + y_at(d) * A_ROWS, A_ROWS), :].astype(F32)
+        total = cache_f[rows_at(ix * A_PIECE + y_at(d) * A_ROWS, A_ROWS), :]
         for k in range(1, NX):
             await_recv(ax_buf.at[k - 1, d], a1_send.at[k - 1, d], a1_recv.at[k - 1, d])
             total = total + ax_buf[k - 1, d].astype(F32)
@@ -631,7 +632,7 @@
         pltpu.SMEM((5, 8, 128), I32),
         vmem((FLAT, DIM), F32),
         vmem((GROUPS, ROWS, 128), F32),
-        vmem((64, 128), F32),
+        vmem((GROUPS, ROWS, 128), BF16),
         vmem((64, 128), F32),
         vmem((64, 128), F32),
         vmem((OWNERS, 8, 128), F32),

time: 79.4 us -> 79.6 us (level)
  the two profiles are of different devices: /device:TPU:1 before, /device:TPU:16 now
where the time goes in v7:
time: 79.6 us; the launch traced here: 79.3 us
  Pallas kernels  78.7 us (99%)
    pallas_call x1, Pallas kernels, call(): pl.pallas_call(kernel, out_shape=out_shape, in_specs=in_specs, out_specs=...  76.7 us
    pallas_call x1, Pallas kernels, shards(): pl.pallas_call(result_kernel, out_shape=[shape(x.shape, x.dtype) for x in...  2.04 us

profile of v7, /device:TPU:16, one launch (start us, length us, event | category | flops | bytes accessed | tf_op | source)
XLA Modules:
  0.0 79.3 jit_solution(1715887770568827720)
XLA Ops:
  0.6 76.7 %shard_map.85 = (bf16[128,768]{1,0:T(8,128)(2,1)}, f32[48,128]{1,0:T(8,128)}, bf16[2880,128]{1,0:T(8,128)(2,1)}) custom-call(bf16[128,768]{1,0:T(8,128)(2,1)} %bitcast.7, bf16[48,128]{1,0:T(8,128)(2,1)} %weight_ref.1, bf16[180,16,128]{2,1,0:T(8,128)(2,1)} %bitcast.6, s32[16]{0:T(128)} %len_ref.1, s32[4,16]{1,0:T(4,128)} %ids.1, s32[256]{0:T(256)} %owner_of.1), custom_call_target="tpu_custom_call" | custom-call | tf_op jit(solution)/shard_map/pallas_call | solution.py:599
  77.3 2.0 %shard_map.86 = (bf16[128,768]{1,0:T(8,128)(2,1)}, f32[48,128]{1,0:T(8,128)}, bf16[2880,128]{1,0:T(8,128)(2,1)}) custom-call(bf16[128,768]{1,0:T(8,128)(2,1)} %get-tuple-element.9.hid, f32[48,128]{1,0:T(8,128)} %get-tuple-element.10.wg, bf16[2880,128]{1,0:T(8,128)(2,1)} %get-tuple-element.11.cache), custom_call_target="tpu_custom_call" | custom-call | tf_op jit(solution)/shard_map/pallas_call | solution.py:693
